TPU v7x, 32 devices: a whole 2x2x4 slice. The times are simulated.
32 devices in a mesh: seq: 8 (over z, x), head: 4 (over y, core).
Axes of the slice: x: 2, y: 2, z: 4, core: 2. Of those that a mesh axis runs over, the one named last changes fastest.
Arguments:
- hidden_in: bfloat16 [32768, 1024], P('seq'), may hold values from -6 to 6
- norm_gain: bfloat16 [1024], replicated, may hold values from 0.099609375 to 1.8984375
- gate_weight: bfloat16 [1024, 2048], P(None, 'head'), may hold values from -0.1875 to 0.1875
- value_weight: bfloat16 [1024, 2048], P(None, 'head'), may hold values from -0.375 to 0.375
- state_weight: bfloat16 [1024, 256], replicated, may hold values from -0.1875 to 0.1875
- step_weight: bfloat16 [1024, 32], P(None, 'head'), may hold values from -0.1875 to 0.1875
- step_bias: float32 [32], P('head'), may hold values from -1 to 1
- decay_log: float32 [32], P('head'), may hold values from -16 to -3
- skip_gain: float32 [32], P('head'), may hold values from 0.5 to 1.5
- conv_value: bfloat16 [4, 2048], P(None, 'head'), may hold values from -3 to 3
- conv_state: bfloat16 [4, 256], replicated, may hold values from -3 to 3
- output_gain: bfloat16 [2048], P('head'), may hold values from 0.099609375 to 1.8984375
- output_weight: bfloat16 [2048, 1024], P('head'), may hold values from -0.125 to 0.125
- piece_lengths: int32 [16], replicated, may hold values from 1 to 16384, 32768 in all
Outputs:
- block_out: bfloat16 [32768, 1024], P(('seq', 'head'))
Inputs may be any that keep to these rules, and one draw needn't show every extreme that they name: `piece_lengths`: the lengths sum to 32768; the pieces lie end to end from position 0.
All inputs are finite; a program needn't handle non-finite values.
Results may differ from a plain program's by a relative error of at most 0.018.
Values may be sent and summed in bfloat16 or wider, within the bound.
No kernel may reach another device: no remote copies, remote signals or barrier semaphores. Data moves between devices by JAX's collectives and lax.ppermute only.
A program may use at most 128 MiB of HBM per device.

v0:
```python
import functools

import jax
import jax.numpy as jnp
from jax import lax
from jax.experimental import pallas as pl
from jax.experimental.pallas import tpu as pltpu
from jax.sharding import PartitionSpec as P

HEAD_DIM = 64
STATE = 128
CONV = 4
BLOCK = 256
HALO = 16
LANES = 128
SAFE = 40.0
EPSILON = 1e-05
VMEM_LIMIT = 56 * 1024 * 1024

f32 = jnp.float32
bf16 = jnp.bfloat16


def dot(a, b):
    return jnp.dot(a, b, preferred_element_type=f32)


def dot_first(a, b):
    return lax.dot_general(a, b, (((0,), (0,)), ((), ())), preferred_element_type=f32)


def dot_last(a, b):
    return lax.dot_general(a, b, (((1,), (1,)), ((), ())), preferred_element_type=f32)


def iota(shape, dim):
    return lax.broadcasted_iota(jnp.int32, shape, dim)


def normalise(rows, gain):
    wide = rows.astype(f32)
    scale = lax.rsqrt(jnp.mean(wide * wide, axis=-1, keepdims=True) + EPSILON)
    return (wide * scale * gain).astype(bf16)


def split_halves(x):
    high = x.astype(bf16)
    low = (x - high.astype(f32)).astype(bf16)
    return high, low


def spread(factors, first, columns):
    pick = (iota((2 * LANES, columns), 0) & (LANES - 1)) == lax.div(
        iota((2 * LANES, columns), 1), HEAD_DIM
    ) + first
    return dot(factors, pick.astype(bf16))


def running_sum(x):
    lower = (iota((BLOCK, BLOCK), 0) >= iota((BLOCK, BLOCK), 1)).astype(bf16)
    high, low = split_halves(x)
    return dot(lower, high) + dot(lower, low)


def start_at(starts, count, row):
    found = starts[0]
    for k in range(1, count):
        s = starts[k]
        found = jnp.where(s <= row, jnp.maximum(found, s), found)
    return found


def start_after(starts, count, row):
    found = starts[count - 1]
    for k in range(count - 1):
        s = starts[k]
        found = jnp.where(s > row, jnp.minimum(found, s), found)
    return found


def has_cut(starts, count, low, high):
    found = jnp.int32(0)
    for k in range(count):
        s = starts[k]
        found = found | jnp.where((s >= low) & (s <= high), 1, 0)
    return found > 0


def row_bounds(starts, count, first):
    rows = iota((BLOCK, 1), 0) + first
    begin = jnp.zeros((BLOCK, 1), jnp.int32)
    end = jnp.zeros((BLOCK, 1), jnp.int32) + starts[count - 1]
    for k in range(count):
        s = starts[k]
        begin = jnp.where(s <= rows, jnp.maximum(begin, s), begin)
        end = jnp.where(s > rows, jnp.minimum(end, s), end)
    return rows, begin, end


def convolve(win, taps, columns, bounds, put):
    wide = LANES if columns % LANES == 0 else columns
    for at in range(0, columns, wide):
        cols = pl.ds(at, wide)

        def row(d):
            return win[pl.ds(HALO + d, BLOCK), cols]

        centre = taps[CONV - 1 : CONV, cols] * row(0)
        halves = []
        for sign in (-1, 1):
            total = centre
            for d in range(1, CONV):
                term = taps[CONV - 1 - d : CONV - d, cols] * row(sign * d)
                if bounds is not None:
                    rows, begin, end = bounds
                    inside = rows - d >= begin if sign < 0 else rows + d < end
                    term = jnp.where(inside, term, 0.0)
                total = total + term
            halves.append(total * jnp.tanh(total) + total)
        put(cols, halves[0], halves[1])


def convolve_block(win, taps, columns, starts, count, first, put):
    cut = has_cut(starts, count, first - (CONV - 2), first + BLOCK + CONV - 2)

    @pl.when(jnp.logical_not(cut))
    def _():
        convolve(win, taps, columns, None, put)

    @pl.when(cut)
    def _():
        convolve(win, taps, columns, row_bounds(starts, count, first), put)


def project_kernel(inner, heads, hidden, gain, value_w, state_w, step_w, bias, mix, steps, joined):
    @pl.when(pl.program_id(0) == 0)
    def _():
        joined[:, :inner] = value_w[...]
        joined[:, inner : inner + STATE] = state_w[...]
        joined[:, inner + STATE :] = step_w[...]

    normed = normalise(hidden[...], gain[...])
    out = dot(normed, joined[...])
    mix[...] = out[:, : inner + STATE].astype(bf16)
    raw = out[:, inner + STATE :] + bias[...]
    steps[...] = jnp.maximum(raw, 0.0) + jnp.log1p(jnp.exp(-jnp.abs(raw)))


def state_kernel(
    inner,
    count,
    places,
    info,
    mix,
    before,
    after,
    halo,
    gain,
    value_w,
    state_w,
    steps,
    rate,
    taps,
    ends,
    begins,
    passes,
    sent,
    edge,
    win,
    xf,
    xb,
    sums,
    total_f,
    total_b,
):
    quarter = pl.program_id(0)
    quarters = pl.num_programs(0)
    rows = mix.shape[0]
    blocks = rows // BLOCK
    columns = inner + STATE
    first = info[count] + quarter * rows

    @pl.when(quarter == 0)
    def _():
        normed = normalise(halo[...], gain[...])
        edge[:, :inner] = dot(normed, value_w[...]).astype(bf16).astype(f32)
        edge[:, inner:] = dot(normed, state_w[...]).astype(bf16).astype(f32)
        total_f[...] = jnp.zeros_like(total_f)
        total_b[...] = jnp.zeros_like(total_b)
        total_b[STATE : STATE + 1] = jnp.ones((1, inner), f32)
        total_f[STATE : STATE + 1] = jnp.ones((1, inner), f32)

    total = jnp.zeros((1, LANES), f32)
    for c in range(blocks):
        at = pl.ds(c * BLOCK, BLOCK)
        part = running_sum(-steps[at, :] * rate[...]) + total
        sums[at, :] = part
        total = part[BLOCK - 1 : BLOCK]

    last_start = start_at(info, count, first + rows - 1)
    first_end = start_after(info, count, first)

    end_state = jnp.zeros((STATE, inner), f32)
    begin_state = jnp.zeros((STATE, inner), f32)
    for c in range(blocks):
        at = pl.ds(c * BLOCK, BLOCK)
        win[HALO : HALO + BLOCK, :] = mix[at, :].astype(f32)
        if c == 0:
            win[:HALO, :] = jnp.where(quarter == 0, edge[:HALO], before[...].astype(f32))
        else:
            win[:HALO, :] = mix[c * BLOCK - HALO : c * BLOCK, :].astype(f32)
        if c == blocks - 1:
            win[HALO + BLOCK :, :] = jnp.where(
                quarter == quarters - 1, edge[HALO:], after[...].astype(f32)
            )
        else:
            win[HALO + BLOCK :, :] = mix[(c + 1) * BLOCK : (c + 1) * BLOCK + HALO, :].astype(f32)

        def put(cols, forward, backward):
            xf[:, cols] = forward
            xb[:, cols] = backward

        here = first + c * BLOCK
        convolve_block(win, taps, columns, info, count, here, put)
        dt = steps[at, :]
        inclusive = sums[at, :]
        weight_f = dt * jnp.exp(total - inclusive)
        weight_b = dt * jnp.exp(inclusive + dt * rate[...])
        position = iota((BLOCK, 1), 0) + here
        spread_f = spread(jnp.concatenate(split_halves(weight_f), axis=1), 0, inner)
        spread_b = spread(jnp.concatenate(split_halves(weight_b), axis=1), 0, inner)
        write_f = jnp.where(position >= last_start, xf[:, inner:], 0.0).astype(bf16)
        write_b = jnp.where(position < first_end, xb[:, inner:], 0.0).astype(bf16)
        end_state += dot_first(write_f, (xf[:, :inner] * spread_f).astype(bf16))
        begin_state += dot_first(write_b, (xb[:, :inner] * spread_b).astype(bf16))

    ends[0] = end_state
    begins[0] = begin_state
    decay = spread(
        jnp.concatenate(split_halves(jnp.broadcast_to(jnp.exp(total), (8, LANES))), axis=1), 0, inner
    )
    pass_f = jnp.where(last_start < first, decay, 0.0)
    pass_b = jnp.where(first_end > first + rows, decay, 0.0)
    passes[0, :8] = pass_f
    passes[0, 8:] = pass_b
    through_f = total_f[STATE : STATE + 1]
    through_b = total_b[STATE : STATE + 1]
    total_f[:STATE] = pass_f[:1] * total_f[:STATE] + end_state
    total_b[:STATE] = total_b[:STATE] + through_b * begin_state
    total_f[STATE : STATE + 1] = through_f * pass_f[:1]
    total_b[STATE : STATE + 1] = through_b * pass_b[:1]

    @pl.when(quarter == quarters - 1)
    def _():
        place = info[count + 1]
        for total_ref, later in ((total_f, True), (total_b, False)):
            state = total_ref[:STATE].astype(bf16)
            high, low = split_halves(total_ref[STATE : STATE + 1])
            pad = jnp.zeros((HALO - 2, inner), f32)
            extra = jnp.concatenate([high.astype(f32), low.astype(f32), pad], axis=0).astype(bf16)

            def fill(p, carry):
                @pl.when((p > place) if later else (p <= place))
                def _():
                    sent[p, :STATE] = state
                    sent[p, STATE:] = extra

                return carry

            lax.fori_loop(0, places, fill, 0)


def carry_kernel(places, quarters, count, info, got, ends, begins, passes, out):
    place = info[count + 1]
    shape = ends.shape[1:]

    def step(p, state):
        decay = got[p, STATE : STATE + HALO].astype(f32)
        return (decay[0:1] + decay[1:2]) * state + got[p, :STATE].astype(f32)

    def forward(p, state):
        return step(p, state)

    def backward(p, state):
        return step(places - 1 - p, state)

    state = lax.fori_loop(0, place, forward, jnp.zeros(shape, f32))
    for q in range(quarters):
        out[q, 0] = state.astype(bf16)
        state = passes[q, 0:1] * state + ends[q]
    state = lax.fori_loop(0, places - 1 - place, backward, jnp.zeros(shape, f32))
    for q in reversed(range(quarters)):
        out[q, 1] = state.astype(bf16)
        state = passes[q, 8:9] * state + begins[q]


def shared_kernel(
    heads,
    count,
    info,
    hidden,
    gain,
    state_w,
    step_w,
    bias,
    rate,
    taps,
    normed_out,
    factors,
    reach,
    raw,
    raw_t,
    mix_f,
    mix_b,
    write_f,
    write_b,
    read_f,
    read_b,
    enter_f,
    enter_b,
    flags,
    wide,
    win,
    xf,
    xb,
):
    rows = hidden.shape[0] - 2 * HALO
    blocks = rows // BLOCK
    first = info[count + 2]
    normed_out[...] = normalise(hidden[...], gain[...])
    wide[...] = dot(normed_out[...], state_w[...]).astype(bf16).astype(f32)
    kind = lax.div(iota((1, LANES), 1), heads)
    totals = []
    for c in range(blocks):
        at = pl.ds(c * BLOCK, BLOCK)
        step_raw = dot(normed_out[pl.ds(HALO + c * BLOCK, BLOCK), :], step_w[...]) + bias[...]
        dt = jnp.maximum(step_raw, 0.0) + jnp.log1p(jnp.exp(-jnp.abs(step_raw)))
        log_step = -dt * rate[...]
        upto = running_sum(log_step)
        total = upto[BLOCK - 1 : BLOCK]
        onward = total - upto + log_step
        totals.append(total)
        flags[c] = jnp.where(jnp.max(-total) > SAFE, 1, 0)
        value = jnp.where(kind == 0, upto, jnp.where(kind == 1, dt, jnp.where(kind == 2, onward, total)))
        raw[at, :] = value
        raw_t[c] = jnp.transpose(value)
        power = jnp.where(
            kind == 0, upto, jnp.where(kind == 1, -upto, jnp.where(kind == 2, onward, -onward))
        )
        factor = jnp.exp(jnp.minimum(power, SAFE)) * jnp.where((kind & 1) == 1, dt, 1.0)
        factors[at, :] = jnp.concatenate(split_halves(factor), axis=1)

    zero = jnp.zeros((1, LANES), f32)
    ahead = [zero]
    for c in range(blocks - 1):
        ahead.append(ahead[-1] + totals[c])
    behind = [zero]
    for c in reversed(range(1, blocks)):
        behind.insert(0, behind[0] + totals[c])
    quarter_end = start_after(info, count, first - 1)
    quarter_start = start_at(info, count, first + rows)
    for c in range(blocks):
        at = pl.ds(c * BLOCK, BLOCK)
        value = raw[at, :]
        power = jnp.where(kind == 0, value + ahead[c], value + behind[c])
        factor = jnp.where((kind & 1) == 0, jnp.exp(jnp.minimum(power, 0.0)), 0.0)
        reach[at, :] = jnp.concatenate(split_halves(factor), axis=1)

        here = first + c * BLOCK
        win[...] = wide[pl.ds(c * BLOCK, BLOCK + 2 * HALO), :]

        def put(cols, forward, backward):
            xf[:, cols] = forward
            xb[:, cols] = backward

        convolve_block(win, taps, 2 * STATE, info, count, here, put)
        position, begin, end = row_bounds(info, count, here)
        other = iota((BLOCK, BLOCK), 1) + here
        for x, mix, write, read, enter, ahead_of in (
            (xf, mix_f, write_f, read_f, enter_f, True),
            (xb, mix_b, write_b, read_b, enter_b, False),
        ):
            writes = x[:, :STATE]
            reads = x[:, STATE:]
            inner_product = dot_last(reads.astype(bf16), writes.astype(bf16))
            if ahead_of:
                allowed = (other <= position) & (other >= begin)
                keep = position >= start_at(info, count, here + BLOCK - 1)
                opened = position < start_after(info, count, here - 1)
                entered = position < quarter_end
            else:
                allowed = (other >= position) & (other < end)
                keep = position < start_after(info, count, here)
                opened = position >= start_at(info, count, here + BLOCK)
                entered = position >= quarter_start
            mix[c] = jnp.where(allowed, inner_product, 0.0).astype(bf16)
            write[at, :] = jnp.where(keep, writes, 0.0).astype(bf16)
            read[at, :] = jnp.where(opened, reads, 0.0).astype(bf16)
            enter[at, :] = jnp.where(entered, reads, 0.0).astype(bf16)


def group_kernel(
    group,
    group_heads,
    heads,
    count,
    info,
    flags,
    normed,
    value_w,
    gate_w,
    taps,
    skip,
    factors,
    raw,
    raw_t,
    mix_f,
    mix_b,
    write_f,
    write_b,
    read_f,
    read_b,
    out_f,
    out_b,
    gate_out,
    win,
    xf,
    xb,
    acc,
    state,
):
    inner = value_w.shape[1]
    rows = out_f.shape[0]
    blocks = rows // BLOCK
    first = info[count + 2]
    offset = group * group_heads

    def direction(c, x, mix, write, read, out, kind, edge_row, passing):
        at = pl.ds(pl.multiple_of(c * BLOCK, BLOCK), BLOCK)
        here_factors = factors[at, :]
        grow = spread(here_factors, kind * heads + offset, inner)
        decay = grow[edge_row : edge_row + 1]
        through = jnp.where(passing, 1.0, 0.0)
        flag = flags[c]
        carried = state[...]
        from_state = dot(read[at, :], carried.astype(bf16))

        @pl.when(flag == 0)
        def _():
            scaled = (x[...] * spread(here_factors, (kind + 1) * heads + offset, inner)).astype(bf16)
            total = dot(mix[c], scaled) + from_state
            out[at, :] = (total * grow + skip[...] * x[...]).astype(bf16)
            state[...] = decay * (dot_first(write[at, :], scaled) + through * carried)

        @pl.when(flag != 0)
        def _():
            pairs = mix[c].astype(f32)
            lane = iota((1, LANES), 1)
            half = iota((1, LANES), 1) >= HEAD_DIM
            values = raw[at, :]

            def pair(p, unused):
                cols = pl.ds(pl.multiple_of(p * LANES, LANES), LANES)
                x_pair = x[:, cols].astype(bf16)
                sums = []
                for side in range(LANES // HEAD_DIM):
                    head = kind * heads + offset + p * (LANES // HEAD_DIM) + side
                    down = jnp.sum(jnp.where(lane == head, values, 0.0), axis=1, keepdims=True)
                    across = raw_t[c, pl.ds(head, 1), :]
                    head_steps = raw_t[c, pl.ds(head - kind * heads + heads, 1), :]
                    table = pairs * jnp.exp(jnp.minimum(down - across, 0.0)) * head_steps
                    sums.append(dot(table.astype(bf16), x_pair))
                acc[:, cols] = jnp.where(half, sums[1], sums[0])
                return unused

            lax.fori_loop(0, inner // LANES, pair, 0)
            out[at, :] = (acc[...] + grow * from_state + skip[...] * x[...]).astype(bf16)
            edge_values = values[edge_row : edge_row + 1]
            step_lane = pltpu.roll(values, (kind - 1) * heads % LANES, 1)
            weight = jnp.where(
                lax.div(lane, heads) == kind,
                step_lane * jnp.exp(jnp.minimum(edge_values - values, 0.0)),
                0.0,
            )
            weights = jnp.concatenate(split_halves(weight), axis=1)
            scaled = (x[...] * spread(weights, kind * heads + offset, inner)).astype(bf16)
            state[...] = dot_first(write[at, :], scaled) + through * decay * carried

    state[...] = jnp.zeros_like(state)

    def ascend(c, unused):
        near = pl.ds(pl.multiple_of(c * BLOCK, BLOCK), BLOCK + 2 * HALO)
        at = pl.ds(pl.multiple_of(c * BLOCK, BLOCK), BLOCK)
        here = first + c * BLOCK
        rows_here = normed[near, :]
        win[...] = dot(rows_here, value_w[...]).astype(bf16).astype(f32)
        gate = dot(rows_here[HALO : HALO + BLOCK], gate_w[...]).astype(bf16).astype(f32) * 0.5
        gate_out[at, :] = (gate * jnp.tanh(gate) + gate).astype(bf16)

        def put(cols, forward, backward):
            xf[:, cols] = forward
            xb[c, :, cols] = backward

        convolve_block(win, taps, inner, info, count, here, put)
        passing = start_at(info, count, here + BLOCK - 1) < here
        direction(c, xf, mix_f, write_f, read_f, out_f, 0, BLOCK - 1, passing)
        return unused

    lax.fori_loop(0, blocks, ascend, 0)
    state[...] = jnp.zeros_like(state)

    def descend(k, unused):
        c = blocks - 1 - k
        here = first + c * BLOCK
        passing = start_after(info, count, here) > here + BLOCK
        direction(c, xb.at[c], mix_b, write_b, read_b, out_b, 2, 0, passing)
        return unused

    lax.fori_loop(0, blocks, descend, 0)


def finish_kernel(groups, group_heads, heads, count, info, *refs):
    hidden, reach, enter_f, enter_b, carries, gains = refs[:6]
    refs = refs[6:]
    out_f, out_b, gates, weights = (refs[k * groups : (k + 1) * groups] for k in range(4))
    out, held_f, held_b = refs[4 * groups :]
    me = info[count + 3]
    inner = weights[0].shape[0]
    here_reach = reach[...]
    sums = [jnp.zeros((BLOCK, 1), f32), jnp.zeros((BLOCK, 1), f32)]
    for g in range(groups):
        gate = gates[g][...].astype(f32)
        for k, (base, enter, held) in enumerate(((out_f, enter_f, held_f), (out_b, enter_b, held_b))):
            grow = spread(here_reach, 2 * k * heads + g * group_heads, inner)
            full = base[g][...].astype(f32) + grow * dot(enter[...], carries[me ^ g, k])
            gated = full * gate
            held[:, g * inner : (g + 1) * inner] = gated
            sums[k] = sums[k] + jnp.sum(gated * gated, axis=1, keepdims=True)
    scale_f, scale_b = (lax.rsqrt(s / (groups * inner) + EPSILON) for s in sums)
    total = hidden[...].astype(f32)
    for g in range(groups):
        cols = slice(g * inner, (g + 1) * inner)
        combined = (held_f[:, cols] * scale_f + held_b[:, cols] * scale_b) * gains[g : g + 1]
        total = total + dot(combined.astype(bf16), weights[g][...])
    out[...] = total.astype(bf16)


def whole(shape):
    return pl.BlockSpec(shape, lambda *_: (0,) * len(shape))


def struct(shape, dtype):
    return jax.ShapeDtypeStruct(shape, dtype)


def call(kernel, grid, scalars, arrays, in_specs, out_shape, out_specs, scratch, name):
    return pl.pallas_call(
        kernel,
        grid_spec=pltpu.PrefetchScalarGridSpec(
            num_scalar_prefetch=len(scalars),
            grid=grid,
            in_specs=in_specs,
            out_specs=out_specs,
            scratch_shapes=scratch,
        ),
        out_shape=out_shape,
        compiler_params=pltpu.CompilerParams(
            dimension_semantics=("arbitrary",) * len(grid), vmem_limit_bytes=VMEM_LIMIT
        ),
        name=name,
    )(*scalars, *arrays)


def swap(x, axis, distance):
    return lax.ppermute(x, axis, [(i, i ^ distance) for i in range(lax.axis_size(axis))])


def gather_near(x, groups):
    held = [None] * groups
    held[0] = x
    for k in range(2, groups, 2):
        held[k] = swap(x, "head", k)
    for k in range(1, groups, 2):
        held[k] = swap(held[k - 1], "head", 1)
    return held


def local(
    hidden_in,
    norm_gain,
    gate_weight,
    value_weight,
    state_weight,
    step_weight,
    step_bias,
    decay_log,
    skip_gain,
    conv_value,
    conv_state,
    output_gain,
    output_weight,
    piece_lengths,
):
    tokens, width = hidden_in.shape
    group_heads = step_bias.shape[0]
    inner = value_weight.shape[1]
    groups = lax.axis_size("head")
    places = lax.axis_size("seq")
    heads = group_heads * groups
    me = lax.axis_index("head")
    place = lax.axis_index("seq")
    rows = tokens // groups
    blocks = rows // BLOCK
    count = piece_lengths.shape[0] + 1

    up = [(i, i + 1) for i in range(places - 1)]
    down = [(i + 1, i) for i in range(places - 1)]
    before = lax.ppermute(hidden_in[-HALO:], "seq", up)
    after = lax.ppermute(hidden_in[:HALO], "seq", down)
    values = gather_near(value_weight, groups)
    gates = gather_near(gate_weight, groups)
    outs = gather_near(output_weight, groups)
    packed = jnp.concatenate(
        [
            conv_value.astype(f32).reshape(-1),
            output_gain.astype(f32),
            step_weight.astype(f32).reshape(-1),
            step_bias,
            decay_log,
            skip_gain,
        ]
    )
    packed = lax.all_gather(packed, "head")
    packed = jnp.take(packed, me ^ jnp.arange(groups), axis=0)
    cuts = [CONV * inner, inner, width * group_heads, group_heads, group_heads, group_heads]
    parts, at = [], 0
    for size in cuts:
        parts.append(packed[:, at : at + size])
        at += size
    taps_all = parts[0].reshape(groups, CONV, inner) * 0.5
    gains_all = parts[1]
    step_all = jnp.transpose(parts[2].reshape(groups, width, group_heads), (1, 0, 2)).reshape(width, heads)
    kinds = LANES // heads
    step_all = jnp.tile(step_all.astype(bf16), (1, kinds))
    bias_all = jnp.tile(parts[3].reshape(1, heads), (1, kinds))
    rate_all = jnp.tile(jnp.exp(parts[4]).reshape(1, heads), (1, kinds))
    skip_all = jnp.repeat(parts[5], HEAD_DIM, axis=1)

    starts = jnp.concatenate([jnp.zeros((1,), jnp.int32), jnp.cumsum(piece_lengths).astype(jnp.int32)])
    info = jnp.concatenate(
        [
            starts,
            jnp.stack([place * tokens, place, place * tokens + me * rows, me]).astype(jnp.int32),
        ]
    )
    gain = norm_gain.astype(f32).reshape(1, width)
    pad = ((0, 0), (0, LANES - group_heads))
    taps_own = jnp.concatenate([conv_value, conv_state[:, :STATE]], axis=1).astype(f32) * 0.5

    tile = min(512, rows)
    columns = inner + STATE
    mix, steps = call(
        functools.partial(project_kernel, inner, group_heads),
        (tokens // tile,),
        (),
        (
            hidden_in,
            gain,
            value_weight,
            state_weight,
            jnp.pad(step_weight, pad),
            jnp.pad(step_bias.reshape(1, -1), pad),
        ),
        [
            pl.BlockSpec((tile, width), lambda i: (i, 0)),
            whole((1, width)),
            whole((width, inner)),
            whole((width, STATE)),
            whole((width, LANES)),
            whole((1, LANES)),
        ],
        [struct((tokens, columns), bf16), struct((tokens, LANES), f32)],
        [pl.BlockSpec((tile, columns), lambda i: (i, 0)), pl.BlockSpec((tile, LANES), lambda i: (i, 0))],
        [pltpu.VMEM((width, columns + LANES), bf16)],
        "project",
    )
    per = rows // HALO
    ends, begins, passes, sent = call(
        functools.partial(state_kernel, inner, count, places),
        (groups,),
        (info,),
        (
            mix,
            mix,
            mix,
            jnp.concatenate([before, after]),
            gain,
            value_weight,
            state_weight,
            steps,
            jnp.pad(jnp.exp(decay_log).reshape(1, -1), pad),
            taps_own,
        ),
        [
            pl.BlockSpec((rows, columns), lambda i, _: (i, 0)),
            pl.BlockSpec((HALO, columns), lambda i, _: (jnp.maximum(i * per - 1, 0), 0)),
            pl.BlockSpec(
                (HALO, columns), lambda i, _: (jnp.minimum((i + 1) * per, tokens // HALO - 1), 0)
            ),
            whole((2 * HALO, width)),
            whole((1, width)),
            whole((width, inner)),
            whole((width, STATE)),
            pl.BlockSpec((rows, LANES), lambda i, _: (i, 0)),
            whole((1, LANES)),
            whole((CONV, columns)),
        ],
        [
            struct((groups, STATE, inner), f32),
            struct((groups, STATE, inner), f32),
            struct((groups, 16, inner), f32),
            struct((places, STATE + HALO, inner), bf16),
        ],
        [
            pl.BlockSpec((1, STATE, inner), lambda i, _: (i, 0, 0)),
            pl.BlockSpec((1, STATE, inner), lambda i, _: (i, 0, 0)),
            pl.BlockSpec((1, 16, inner), lambda i, _: (i, 0, 0)),
            whole((places, STATE + HALO, inner)),
        ],
        [
            pltpu.VMEM((2 * HALO, columns), f32),
            pltpu.VMEM((BLOCK + 2 * HALO, columns), f32),
            pltpu.VMEM((BLOCK, columns), f32),
            pltpu.VMEM((BLOCK, columns), f32),
            pltpu.VMEM((rows, LANES), f32),
            pltpu.VMEM((STATE + 8, inner), f32),
            pltpu.VMEM((STATE + 8, inner), f32),
        ],
        "states",
    )
    got = lax.all_to_all(sent, "seq", split_axis=0, concat_axis=0, tiled=True)

    own_first = me * rows
    own = lax.dynamic_slice_in_dim(hidden_in, own_first, rows, 0)
    above = lax.dynamic_slice_in_dim(hidden_in, jnp.maximum(own_first - HALO, 0), HALO, 0)
    below = lax.dynamic_slice_in_dim(hidden_in, jnp.minimum(own_first + rows, tokens - HALO), HALO, 0)
    near = jnp.concatenate(
        [jnp.where(me == 0, before, above), own, jnp.where(me == groups - 1, after, below)]
    )
    long = rows + 2 * HALO
    square = struct((blocks, BLOCK, BLOCK), bf16)
    thin = struct((rows, STATE), bf16)
    shapes = [
        struct((long, width), bf16),
        struct((rows, 2 * LANES), bf16),
        struct((rows, 2 * LANES), bf16),
        struct((rows, LANES), f32),
        struct((blocks, LANES, BLOCK), f32),
        square,
        square,
        thin,
        thin,
        thin,
        thin,
        thin,
        thin,
        struct((blocks,), jnp.int32),
    ]
    shared = call(
        functools.partial(shared_kernel, heads, count),
        (1,),
        (info,),
        (near, gain, state_weight, step_all, bias_all, rate_all, conv_state.astype(f32) * 0.5),
        [
            whole((long, width)),
            whole((1, width)),
            whole((width, 2 * STATE)),
            whole((width, LANES)),
            whole((1, LANES)),
            whole((1, LANES)),
            whole((CONV, 2 * STATE)),
        ],
        shapes,
        [whole(s.shape) for s in shapes[:-1]] + [pl.BlockSpec(memory_space=pltpu.SMEM)],
        [
            pltpu.VMEM((long, 2 * STATE), f32),
            pltpu.VMEM((BLOCK + 2 * HALO, 2 * STATE), f32),
            pltpu.VMEM((BLOCK, 2 * STATE), f32),
            pltpu.VMEM((BLOCK, 2 * STATE), f32),
        ],
        "shared",
    )
    normed, factors, reach, raw, raw_t, mix_f, mix_b, write_f, write_b, read_f, read_b = shared[:11]
    enter_f, enter_b, flags = shared[11:]
    outs_f, outs_b, gate_rows = [], [], []
    for g in range(groups):
        arrays = (
            normed,
            values[g],
            gates[g],
            taps_all[g],
            skip_all[g : g + 1],
            factors,
            raw,
            raw_t,
            mix_f,
            mix_b,
            write_f,
            write_b,
            read_f,
            read_b,
        )
        done = call(
            functools.partial(group_kernel, g, group_heads, heads, count),
            (1,),
            (info, flags),
            arrays,
            [whole(a.shape) for a in arrays],
            [struct((rows, inner), bf16)] * 3,
            [whole((rows, inner))] * 3,
            [
                pltpu.VMEM((BLOCK + 2 * HALO, inner), f32),
                pltpu.VMEM((BLOCK, inner), f32),
                pltpu.VMEM((blocks, BLOCK, inner), f32),
                pltpu.VMEM((BLOCK, inner), f32),
                pltpu.VMEM((STATE, inner), f32),
            ],
            "group%d" % g,
        )
        outs_f.append(done[0])
        outs_b.append(done[1])
        gate_rows.append(done[2])

    entering = call(
        functools.partial(carry_kernel, places, groups, count),
        (1,),
        (info,),
        (got, ends, begins, passes),
        [whole(a.shape) for a in (got, ends, begins, passes)],
        struct((groups, 2, STATE, inner), bf16),
        whole((groups, 2, STATE, inner)),
        [],
        "carries",
    )
    carries = lax.all_to_all(entering, "head", split_axis=0, concat_axis=0, tiled=True)

    def by_block(columns):
        return pl.BlockSpec((BLOCK, columns), lambda i, _: (i, 0))

    return call(
        functools.partial(finish_kernel, groups, group_heads, heads, count),
        (blocks,),
        (info,),
        (own, reach, enter_f, enter_b, carries, gains_all, *outs_f, *outs_b, *gate_rows, *outs),
        [
            by_block(width),
            by_block(2 * LANES),
            by_block(STATE),
            by_block(STATE),
            whole(carries.shape),
            whole(gains_all.shape),
        ]
        + [by_block(inner)] * (3 * groups)
        + [whole((inner, width))] * groups,
        struct((rows, width), bf16),
        by_block(width),
        [pltpu.VMEM((BLOCK, groups * inner), f32), pltpu.VMEM((BLOCK, groups * inner), f32)],
        "finish",
    )


def solution(mesh):
    in_specs = (
        P("seq", None),
        P(),
        P(None, "head"),
        P(None, "head"),
        P(),
        P(None, "head"),
        P("head"),
        P("head"),
        P("head"),
        P(None, "head"),
        P(),
        P("head"),
        P("head", None),
        P(),
    )
    out_specs = P(("seq", "head"), None)
    return jax.shard_map(local, mesh=mesh, in_specs=in_specs, out_specs=out_specs, check_vma=False)
```

profile of v0, /device:TPU:0, one launch (start us, length us, event | category | flops | bytes accessed | tf_op | source)
XLA Modules:
  0.0 239.0 jit_solution(13696715390762328418)
XLA Ops:
  7.0 2.5 %collective-permute-start.4 = (bf16[1024,512]{1,0:T(8,128)(2,1)}, bf16[1024,512]{1,0:T(8,128)(2,1)}, u32[]{:S(2)}, u32[]{:S(2)}) collective-permute-start(bf16[1024,512]{1,0:T(8,128)(2,1)} %value_w.5), channel_id=1, source_target_pairs={{0,2},{1,3},{2,0},{3,1},{4,6},{5,7},{6,4},{7,5},{8,10},{9,11},{10,... | collective-permute-start | bytes 3145736 | tf_op jit(solution)/shard_map/ppermute | solution.py:575
  10.3 3.4 %collective-permute-start = (bf16[16,1024]{1,0:T(8,128)(2,1)S(1)}, bf16[16,1024]{1,0:T(8,128)(2,1)S(1)}, u32[]{:S(2)}, u32[]{:S(2)}) collective-permute-start(bf16[16,1024]{1,0:T(8,128)(2,1)S(1)} %slice.74), channel_id=1, source_target_pairs={{0,4},{4,8},{8,12},{12,16},{16,20},{20,24},{24,28},{1,5},{5,9},{9,... | collective-permute-start | bytes 98312 | tf_op jit(solution)/shard_map/ppermute | solution.py:618
  15.5 1.2 dynamic-slice
  17.4 1.5 concatenate.17
  20.8 1.5 collective-permute-start.9
  22.9 1.3 convert_multiply_fusion.1.taps
  24.3 1.8 constant_dynamic-slice_fusion.refs_0_
  27.6 1.3 collective-permute-start.1
  31.9 13.5 %project.1 = (bf16[4096,640]{1,0:T(8,128)(2,1)}, f32[4096,128]{1,0:T(8,128)}) custom-call(bf16[4096,1024]{1,0:T(8,128)(2,1)} %hidden.1, f32[1,1024]{1,0:T(1,128)} %bitcast.29, bf16[1024,512]{1,0:T(8,128)(2,1)} %value_w.5, bf16[1024,256]{1,0:T(8,128)(2,1)} %state_w.5, bf16[1024,128]{1,0:T(8,128)(2,1)} %pad.11.step_w, f32[1,128]{1,0:T(1,128)} %pad.12.bias), custom_call_target="tpu_custom_call" | custom-call | tf_op jit(solution)/shard_map/project/pallas_call | solution.py:557
  46.7 25.4 %states.1 = (f32[4,128,512]{2,1,0:T(8,128)}, f32[4,128,512]{2,1,0:T(8,128)}, f32[4,16,512]{2,1,0:T(8,128)}, bf16[8,144,512]{2,1,0:T(8,128)(2,1)}) custom-call(s32[21]{0:T(128)} %concatenate.15.info, bf16[4096,640]{1,0:T(8,128)(2,1)} %get-tuple-element.40.mix.before.after, bf16[4096,640]{1,0:T(8,128)(2,1)} %get-tuple-element.40.mix.before.after, ...), custom_call_target="tpu_custom_call" | custom-call | tf_op jit(solution)/shard_map/states/pallas_call | solution.py:557
  72.1 13.2 %all-to-all-start = ((bf16[8,144,512]{2,1,0:T(8,128)(2,1)}), bf16[8,144,512]{2,1,0:T(8,128)(2,1)S(1)}, u32[]{:S(2)}, u32[]{:S(2)}) async-start(bf16[8,144,512]{2,1,0:T(8,128)(2,1)} %get-tuple-element.42), calls=%async_computation | async-start | bytes 2359296 | tf_op jit(solution)/shard_map/all_to_all | solution.py:741
  86.2 1.5 pad_maximum_fusion.hidden
  87.7 1.1 reshape.150
  91.3 1.2 convert_element_type.32
  95.2 19.4 %all-to-all-done.got = bf16[8,144,512]{2,1,0:T(8,128)(2,1)S(1)} async-done(((bf16[8,144,512]{2,1,0:T(8,128)(2,1)}), bf16[8,144,512]{2,1,0:T(8,128)(2,1)S(1)}, u32[]{:S(2)}, u32[]{:S(2)}) %all-to-all-start) | async-done | bytes 1179680 | tf_op jit(solution)/shard_map/all_to_all | solution.py:741
  114.6 1.0 copy-done.1
  115.6 4.2 %carries.1 = bf16[4,2,128,512]{3,2,1,0:T(8,128)(2,1)} custom-call(s32[21]{0:T(128)} %concatenate.15.info, bf16[8,144,512]{2,1,0:T(8,128)(2,1)} %copy-done.1, f32[4,128,512]{2,1,0:T(8,128)} %get-tuple-element.43.ends, f32[4,128,512]{2,1,0:T(8,128)} %get-tuple-element.44.begins, f32[4,16,512]{2,1,0:T(8,128)} %get-tuple-element.45.passes), custom_call_target="tpu_custom_call" | custom-call | tf_op jit(solution)/shard_map/carries/pallas_call | solution.py:557
  119.8 3.5 %all-to-all-start.1 = ((bf16[4,2,128,512]{3,2,1,0:T(8,128)(2,1)}), bf16[4,2,128,512]{3,2,1,0:T(8,128)(2,1)S(1)}, u32[]{:S(2)}, u32[]{:S(2)}) async-start(bf16[4,2,128,512]{3,2,1,0:T(8,128)(2,1)} %carries.1), calls=%async_computation.1 | async-start | bytes 2097152 | tf_op jit(solution)/shard_map/all_to_all | solution.py:845
  128.8 13.0 %shared.1 = (bf16[1056,1024]{1,0:T(8,128)(2,1)}, bf16[1024,256]{1,0:T(8,128)(2,1)}, bf16[1024,256]{1,0:T(8,128)(2,1)}, f32[1024,128]{1,0:T(8,128)}, f32[4,128,25...) custom-call(s32[21]{0:T(128)} %concatenate.15.info, ...), custom_call_target="tpu_custom_call" | custom-call | tf_op jit(solution)/shard_map/shared/pallas_call | solution.py:557
  141.9 17.8 %group0.1 = (bf16[1024,512]{1,0:T(8,128)(2,1)}, bf16[1024,512]{1,0:T(8,128)(2,1)}, bf16[1024,512]{1,0:T(8,128)(2,1)}) custom-call(s32[21]{0:T(128)} %concatenate.15.info, s32[4]{0:T(128)} %get-tuple-element.46.flags, bf16[1056,1024]{1,0:T(8,128)(2,1)} %get-tuple-element.47.normed, bf16[1024,512]{1,0:T(8,128)(2,1)} %value_w.5, bf16[1024,512]{1,0:T(8,128)(2,1)} %gate_w.1, ...), custom_call_target="tpu_custom_call" | custom-call | tf_op jit(solution)/shard_map/group0/pallas_call | solution.py:557
  159.7 17.8 %group2.1 = (bf16[1024,512]{1,0:T(8,128)(2,1)}, bf16[1024,512]{1,0:T(8,128)(2,1)}, bf16[1024,512]{1,0:T(8,128)(2,1)}) custom-call(s32[21]{0:T(128)} %concatenate.15.info, s32[4]{0:T(128)} %get-tuple-element.46.flags, bf16[1056,1024]{1,0:T(8,128)(2,1)} %get-tuple-element.47.normed, bf16[1024,512]{1,0:T(8,128)(2,1)} %collective-permute-done.4.value_w, ...), custom_call_target="tpu_custom_call" | custom-call | tf_op jit(solution)/shard_map/group2/pallas_call | solution.py:557
  177.5 18.3 %group1.1 = (bf16[1024,512]{1,0:T(8,128)(2,1)}, bf16[1024,512]{1,0:T(8,128)(2,1)}, bf16[1024,512]{1,0:T(8,128)(2,1)}) custom-call(s32[21]{0:T(128)} %concatenate.15.info, s32[4]{0:T(128)} %get-tuple-element.46.flags, bf16[1056,1024]{1,0:T(8,128)(2,1)} %get-tuple-element.47.normed, bf16[1024,512]{1,0:T(8,128)(2,1)} %collective-permute-done.2.value_w, ...), custom_call_target="tpu_custom_call" | custom-call | tf_op jit(solution)/shard_map/group1/pallas_call | solution.py:557
  195.7 18.0 %group3.1 = (bf16[1024,512]{1,0:T(8,128)(2,1)}, bf16[1024,512]{1,0:T(8,128)(2,1)}, bf16[1024,512]{1,0:T(8,128)(2,1)}) custom-call(s32[21]{0:T(128)} %concatenate.15.info, s32[4]{0:T(128)} %get-tuple-element.46.flags, bf16[1056,1024]{1,0:T(8,128)(2,1)} %get-tuple-element.47.normed, bf16[1024,512]{1,0:T(8,128)(2,1)} %collective-permute-done.6.value_w, ...), custom_call_target="tpu_custom_call" | custom-call | tf_op jit(solution)/shard_map/group3/pallas_call | solution.py:557
  215.1 16.8 %finish.1 = bf16[1024,1024]{1,0:T(8,128)(2,1)} custom-call(s32[21]{0:T(128)} %concatenate.15.info, bf16[1024,1024]{1,0:T(8,128)(2,1)} %copy-done, bf16[1024,256]{1,0:T(8,128)(2,1)} %get-tuple-element.37.refs_1_, bf16[1024,128]{1,0:T(8,128)(2,1)} %get-tuple-element.38.refs_2_, bf16[1024,128]{1,0:T(8,128)(2,1)} %get-tuple-element.39.refs_3_, ...), custom_call_target="tpu_custom_call" | custom-call | tf_op jit(solution)/shard_map/finish/pallas_call | solution.py:557
  (96 shorter events, 24.2 us)
Async XLA Ops:
  6.5 81.2 %all-reduce.6.cloned.1.call-start = ((), (), s32[]{:S(2)}) async-start(), calls=%async_computation.2 | async-start | bytes 352256
  6.5 82.9 %collective-permute-start.2 = (bf16[1024,512]{1,0:T(8,128)(2,1)}, bf16[1024,512]{1,0:T(8,128)(2,1)}, u32[]{:S(2)}, u32[]{:S(2)}) collective-permute-start(bf16[1024,512]{1,0:T(8,128)(2,1)} %value_w.5), channel_id=1, source_target_pairs={{0,1},{1,0},{2,3},{3,2},{4,5},{5,4},{6,7},{7,6},{8,9},{9,8},{10,11... | collective-permute-start | bytes 3145736 | tf_op jit(solution)/shard_map/ppermute | solution.py:575
  7.0 82.7 %collective-permute-start.4 = (bf16[1024,512]{1,0:T(8,128)(2,1)}, bf16[1024,512]{1,0:T(8,128)(2,1)}, u32[]{:S(2)}, u32[]{:S(2)}) collective-permute-start(bf16[1024,512]{1,0:T(8,128)(2,1)} %value_w.5), channel_id=1, source_target_pairs={{0,2},{1,3},{2,0},{3,1},{4,6},{5,7},{6,4},{7,5},{8,10},{9,11},{10,... | collective-permute-start | bytes 3145736 | tf_op jit(solution)/shard_map/ppermute | solution.py:575
  10.3 16.5 %collective-permute-start = (bf16[16,1024]{1,0:T(8,128)(2,1)S(1)}, bf16[16,1024]{1,0:T(8,128)(2,1)S(1)}, u32[]{:S(2)}, u32[]{:S(2)}) collective-permute-start(bf16[16,1024]{1,0:T(8,128)(2,1)S(1)} %slice.74), channel_id=1, source_target_pairs={{0,4},{4,8},{8,12},{12,16},{16,20},{20,24},{24,28},{1,5},{5,9},{9,... | collective-permute-start | bytes 98312 | tf_op jit(solution)/shard_map/ppermute | solution.py:618
  19.5 6.6 %copy-start.6 = (bf16[4,512]{1,0:T(4,128)(2,1)S(1)}, bf16[4,512]{1,0:T(4,128)(2,1)}, u32[]{:S(2)}) copy-start(bf16[4,512]{1,0:T(4,128)(2,1)} %param.23) | copy-start | bytes 12292
  19.5 6.6 %slice-start = ((bf16[4,256]{1,0:T(4,128)(2,1)}), bf16[4,128]{1,0:T(4,128)(2,1)S(1)}, s32[]{:S(2)}) async-start(bf16[4,256]{1,0:T(4,128)(2,1)} %param.24), calls=%async_computation.3 | async-start | bytes 2048 | tf_op jit(solution)/shard_map/slice | solution.py:658
  20.2 69.8 %collective-permute-start.5 = (bf16[1024,512]{1,0:T(8,128)(2,1)}, bf16[1024,512]{1,0:T(8,128)(2,1)}, u32[]{:S(2)}, u32[]{:S(2)}) collective-permute-start(bf16[1024,512]{1,0:T(8,128)(2,1)} %gate_w.1), channel_id=1, source_target_pairs={{0,2},{1,3},{2,0},{3,1},{4,6},{5,7},{6,4},{7,5},{8,10},{9,11},{10,... | collective-permute-start | bytes 3145736 | tf_op jit(solution)/shard_map/ppermute | solution.py:575
  20.8 69.5 %collective-permute-start.9 = (bf16[512,1024]{1,0:T(8,128)(2,1)}, bf16[512,1024]{1,0:T(8,128)(2,1)}, u32[]{:S(2)}, u32[]{:S(2)}) collective-permute-start(bf16[512,1024]{1,0:T(8,128)(2,1)} %refs_18_.1), channel_id=1, source_target_pairs={{0,2},{1,3},{2,0},{3,1},{4,6},{5,7},{6,4},{7,5},{8,10},{9,11},{10,... | collective-permute-start | bytes 3145736 | tf_op jit(solution)/shard_map/ppermute | solution.py:575
  24.2 4.7 %copy-start.5 = (bf16[1024,8]{0,1:T(8,128)(2,1)S(1)}, bf16[1024,8]{0,1:T(8,128)(2,1)}, u32[]{:S(2)}) copy-start(bf16[1024,8]{0,1:T(8,128)(2,1)} %param.19) | copy-start | bytes 49156
  24.2 4.9 %copy-start.9 = (s32[16]{0:T(128)S(1)}, s32[16]{0:T(128)}, u32[]{:S(2)}) copy-start(s32[16]{0:T(128)} %param.27) | copy-start | bytes 196
  24.2 5.2 %copy-start.7 = (bf16[1024]{0:T(1024)(128)(2,1)S(1)}, bf16[1024]{0:T(1024)(128)(2,1)}, u32[]{:S(2)}) copy-start(bf16[1024]{0:T(1024)(128)(2,1)} %param.15) | copy-start | bytes 6148
  24.2 5.8 %copy-start.8 = (f32[8]{0:T(128)S(1)}, f32[8]{0:T(128)}, u32[]{:S(2)}) copy-start(f32[8]{0:T(128)} %param.20) | copy-start | bytes 100
  26.1 60.1 %copy-start = (bf16[1024,1024]{1,0:T(8,128)(2,1)}, bf16[1024,1024]{1,0:T(8,128)(2,1)S(1)}, u32[]{:S(2)}) copy-start(bf16[1024,1024]{1,0:T(8,128)(2,1)S(1)} %constant_dynamic-slice_fusion.refs_0_) | copy-start | bytes 6291460
  27.6 18.5 %collective-permute-start.1 = (bf16[16,1024]{1,0:T(8,128)(2,1)S(1)}, bf16[16,1024]{1,0:T(8,128)(2,1)S(1)}, u32[]{:S(2)}, u32[]{:S(2)}) collective-permute-start(bf16[16,1024]{1,0:T(8,128)(2,1)S(1)} %get-tuple-element.74), channel_id=1, source_target_pairs={{4,0},{8,4},{12,8},{16,12},{20,16},{24,20},{28,24},{5,1},{9,5},{13... | collective-permute-start | bytes 98312 | tf_op jit(solution)/shard_map/ppermute | solution.py:619
  46.1 131.4 %collective-permute-start.3 = (bf16[1024,512]{1,0:T(8,128)(2,1)}, bf16[1024,512]{1,0:T(8,128)(2,1)}, u32[]{:S(2)}, u32[]{:S(2)}) collective-permute-start(bf16[1024,512]{1,0:T(8,128)(2,1)} %gate_w.1), channel_id=1, source_target_pairs={{0,1},{1,0},{2,3},{3,2},{4,5},{5,4},{6,7},{7,6},{8,9},{9,8},{10,11... | collective-permute-start | bytes 3145736 | tf_op jit(solution)/shard_map/ppermute | solution.py:575
  72.1 42.4 %all-to-all-start = ((bf16[8,144,512]{2,1,0:T(8,128)(2,1)}), bf16[8,144,512]{2,1,0:T(8,128)(2,1)S(1)}, u32[]{:S(2)}, u32[]{:S(2)}) async-start(bf16[8,144,512]{2,1,0:T(8,128)(2,1)} %get-tuple-element.42), calls=%async_computation | async-start | bytes 2359296 | tf_op jit(solution)/shard_map/all_to_all | solution.py:741
  89.4 124.3 %collective-permute-start.8 = (bf16[512,1024]{1,0:T(8,128)(2,1)}, bf16[512,1024]{1,0:T(8,128)(2,1)S(1)}, u32[]{:S(2)}, u32[]{:S(2)}) collective-permute-start(bf16[512,1024]{1,0:T(8,128)(2,1)} %refs_18_.1), channel_id=1, source_target_pairs={{0,1},{1,0},{2,3},{3,2},{4,5},{5,4},{6,7},{7,6},{8,9},{9,8},{10,11... | collective-permute-start | bytes 3145736 | tf_op jit(solution)/shard_map/ppermute | solution.py:575
  89.7 106.0 %collective-permute-start.6 = (bf16[1024,512]{1,0:T(8,128)(2,1)}, bf16[1024,512]{1,0:T(8,128)(2,1)}, u32[]{:S(2)}, u32[]{:S(2)}) collective-permute-start(bf16[1024,512]{1,0:T(8,128)(2,1)} %collective-permute-done.4.value_w), channel_id=1, source_target_pairs={{0,1},{1,0},{2,3},{3,2},{4,5},{5,4},{6,7},{7,6},{8,9},{9,8},{10,11... | collective-permute-start | bytes 3145736 | tf_op jit(solution)/shard_map/ppermute | solution.py:575
  90.0 105.7 %collective-permute-start.7 = (bf16[1024,512]{1,0:T(8,128)(2,1)}, bf16[1024,512]{1,0:T(8,128)(2,1)}, u32[]{:S(2)}, u32[]{:S(2)}) collective-permute-start(bf16[1024,512]{1,0:T(8,128)(2,1)} %collective-permute-done.5.gate_w), channel_id=1, source_target_pairs={{0,1},{1,0},{2,3},{3,2},{4,5},{5,4},{6,7},{7,6},{8,9},{9,8},{10,11... | collective-permute-start | bytes 3145736 | tf_op jit(solution)/shard_map/ppermute | solution.py:575
  90.2 123.5 %collective-permute-start.10 = (bf16[512,1024]{1,0:T(8,128)(2,1)}, bf16[512,1024]{1,0:T(8,128)(2,1)}, u32[]{:S(2)}, u32[]{:S(2)}) collective-permute-start(bf16[512,1024]{1,0:T(8,128)(2,1)} %collective-permute-done.9.refs_20_), channel_id=1, source_target_pairs={{0,1},{1,0},{2,3},{3,2},{4,5},{5,4},{6,7},{7,6},{8,9},{9,8},{10,11... | collective-permute-start | bytes 3145736 | tf_op jit(solution)/shard_map/ppermute | solution.py:575
  114.6 1.0 copy-start.1
  119.8 94.0 %all-to-all-start.1 = ((bf16[4,2,128,512]{3,2,1,0:T(8,128)(2,1)}), bf16[4,2,128,512]{3,2,1,0:T(8,128)(2,1)S(1)}, u32[]{:S(2)}, u32[]{:S(2)}) async-start(bf16[4,2,128,512]{3,2,1,0:T(8,128)(2,1)} %carries.1), calls=%async_computation.1 | async-start | bytes 2097152 | tf_op jit(solution)/shard_map/all_to_all | solution.py:845
  213.7 1.0 copy-start.3
  213.8 1.4 copy-start.2
  (1 other events, 0.7 us)
Sparse Core Ops, SparseCore 0:
  20.3 31.3 all-reduce.5
where the time goes:
time: 244 us; the launch traced here: 239 us
  Pallas kernels  145 us (59%)
  starting transfers between devices  27.6 us (11%)
  local copies, waits for them, and re-layouts  25.3 us (10%)
  waiting for transfers between devices  19.4 us (8%)
  between operations  14.6 us (6%)
  other arithmetic  7.31 us (3%)
    pallas_call x9, Pallas kernels, call(): pl.pallas_call(kernel, grid_spec=pltpu.PrefetchScalarGridSpec(num_scalar_...  145 us
    all_to_all x1, waiting for transfers between devices, local(): got = lax.all_to_all(sent, 'seq', split_axis=0, concat_axis=0, tiled=True)  19.4 us
    all_to_all x1, starting transfers between devices, local(): got = lax.all_to_all(sent, 'seq', split_axis=0, concat_axis=0, tiled=True)  13.2 us
    ppermute x9, starting transfers between devices, swap(): lax.ppermute(x, axis, [(i, i ^ distance) for i in range(lax.axis_size(axi...  6.15 us
    unnamed x25, local copies, waits for them, and re-layouts  5.11 us
  transfers between devices with their start and end apart: 14, of which 1 were waited for; matrix products, arithmetic and copies ran while one was open for 12% of the time, Pallas kernels for 54%

commit v1 on v0

v1 whole, which is shorter than its diff:
```python
import functools

import jax
import jax.numpy as jnp
from jax import lax
from jax.experimental import pallas as pl
from jax.experimental.pallas import tpu as pltpu
from jax.sharding import PartitionSpec as P

HEAD_DIM = 64
STATE = 128
CONV = 4
BLOCK = 256
HALO = 16
SUB = 8
SPAN = BLOCK // SUB + 1
COVER = SPAN * SUB
WINDOW = BLOCK + 2 * HALO
LANES = 128
SAFE = 40.0
EPSILON = 1e-05
VMEM_LIMIT = 56 * 1024 * 1024

f32 = jnp.float32
bf16 = jnp.bfloat16


def dot(a, b):
    return jnp.dot(a, b, preferred_element_type=f32)


def dot_first(a, b):
    return lax.dot_general(a, b, (((0,), (0,)), ((), ())), preferred_element_type=f32)


def dot_last(a, b):
    return lax.dot_general(a, b, (((1,), (1,)), ((), ())), preferred_element_type=f32)


def iota(shape, dim):
    return lax.broadcasted_iota(jnp.int32, shape, dim)


def normalise(rows, gain):
    wide = rows.astype(f32)
    scale = lax.rsqrt(jnp.mean(wide * wide, axis=-1, keepdims=True) + EPSILON)
    return (wide * scale * gain).astype(bf16)


def split_halves(x):
    high = x.astype(bf16)
    low = (x - high.astype(f32)).astype(bf16)
    return high, low


def picks(first, columns):
    shape = (2 * LANES, columns)
    pick = (iota(shape, 0) & (LANES - 1)) == lax.div(iota(shape, 1), HEAD_DIM) + first
    return pick.astype(bf16)


def side_by_side(tiles):
    return jnp.concatenate([tiles[k, :BLOCK] for k in range(tiles.shape[0])], axis=1)


def tile_up(tiles, at, x):
    for k in range(tiles.shape[0]):
        tiles[k, at] = x[:, k * LANES : (k + 1) * LANES]


def halves_of(x):
    return jnp.concatenate(split_halves(x), axis=1)


def running_sum(x):
    lower = (iota((BLOCK, BLOCK), 0) >= iota((BLOCK, BLOCK), 1)).astype(bf16)
    high, low = split_halves(x)
    return dot(lower, high) + dot(lower, low)


def bounds_of(lengths, pieces):
    starts = [jnp.int32(0)]
    for k in range(pieces):
        starts.append(starts[-1] + lengths[k])
    return starts


def start_at(starts, row):
    found = starts[0]
    for s in starts[1:]:
        found = jnp.where(s <= row, jnp.maximum(found, s), found)
    return found


def start_after(starts, row):
    found = starts[-1]
    for s in starts[:-1]:
        found = jnp.where(s > row, jnp.minimum(found, s), found)
    return found


def has_cut(starts, low, high):
    found = jnp.int32(0)
    for s in starts:
        found = found | jnp.where((s >= low) & (s <= high), 1, 0)
    return found > 0


def piece_bounds(starts, rows):
    begin = jnp.zeros(rows.shape, jnp.int32)
    end = jnp.zeros(rows.shape, jnp.int32) + starts[-1]
    for s in starts:
        begin = jnp.where(s <= rows, jnp.maximum(begin, s), begin)
        end = jnp.where(s > rows, jnp.minimum(end, s), end)
    return begin, end


def convolve(win, offset, taps, room, put):
    offset = offset + HALO
    for tile in range(win.shape[0]):
        cols = pl.ds(tile * LANES, LANES)
        tap = [jnp.broadcast_to(taps[k : k + 1, cols], (SUB, LANES)) for k in range(CONV)]
        near = {
            u: win[tile, pl.ds(offset + u, SUB, stride=SPAN), :] for u in range(1 - CONV, SPAN + CONV - 1)
        }
        for v in range(SPAN):
            centre = tap[CONV - 1] * near[v]
            halves = []
            for sign in (-1, 1):
                total = centre
                for d in range(1, CONV):
                    term = tap[CONV - 1 - d] * near[v + sign * d]
                    if room is not None:
                        left = jnp.broadcast_to(room[sign > 0][:, v : v + 1], (SUB, LANES))
                        term = jnp.where(left >= d, term, 0.0)
                    total = total + term
                halves.append(total * jnp.tanh(total) + total)
            put(tile, pl.ds(v, SUB, stride=SPAN), halves[0], halves[1])


def convolve_block(win, offset, taps, starts, first, put):
    convolve(win, offset, taps, None, put)

    @pl.when(has_cut(starts, first - (CONV - 2), first + BLOCK + CONV - 2))
    def _():
        shape = (SUB, LANES)
        rows = first + iota(shape, 0) * SPAN + iota(shape, 1)
        begin, end = piece_bounds(starts, rows)
        room = ((rows - begin).astype(f32), (end - 1 - rows).astype(f32))
        convolve(win, offset, taps, room, put)


def softplus(x):
    return jnp.maximum(x, 0.0) + jnp.log1p(jnp.exp(-jnp.abs(x)))


def project_kernel(inner, heads, hidden, gain, value_w, state_w, step_w, bias, mix, steps, joined, row):
    @pl.when(pl.program_id(0) == 0)
    def _():
        joined[:, :inner] = value_w[...]
        joined[:, inner : inner + STATE] = state_w[...]
        rows = jnp.concatenate(
            [step_w[...].astype(f32), jnp.zeros((LANES - heads, step_w.shape[1]), f32)], axis=0
        )
        joined[:, inner + STATE :] = jnp.transpose(rows).astype(bf16)
        row[...] = jnp.zeros_like(row)
        row[:, :heads] = bias[...]

    normed = normalise(hidden[...], gain[...].astype(f32))
    out = dot(normed, joined[...])
    mix[...] = out[:, : inner + STATE].astype(bf16)
    steps[...] = softplus(out[:, inner + STATE :] + row[...])


def state_kernel(
    inner,
    heads,
    pieces,
    places,
    lengths,
    info,
    mix,
    before,
    after,
    halo_before,
    halo_after,
    gain,
    value_w,
    state_w,
    steps,
    decay_log,
    conv_value,
    conv_state,
    ends,
    begins,
    passes,
    sent,
    edge,
    win,
    xf,
    xb,
    sums,
    total_f,
    total_b,
    taps,
    rate,
    pick,
):
    quarter = pl.program_id(0)
    quarters = pl.num_programs(0)
    rows = mix.shape[0]
    blocks = rows // BLOCK
    value_tiles = inner // LANES
    starts = bounds_of(lengths, pieces)
    first = info[0] + quarter * rows

    @pl.when(quarter == 0)
    def _():
        for k, halo in enumerate((halo_before, halo_after)):
            normed = normalise(halo[...], gain[...].astype(f32))
            at = pl.ds(k * HALO, HALO)
            edge[at, :inner] = dot(normed, value_w[...]).astype(bf16).astype(f32)
            edge[at, inner:] = dot(normed, state_w[...]).astype(bf16).astype(f32)
        total_f[...] = jnp.zeros_like(total_f)
        total_b[...] = jnp.zeros_like(total_b)
        total_b[STATE : STATE + 1] = jnp.ones((1, inner), f32)
        total_f[STATE : STATE + 1] = jnp.ones((1, inner), f32)
        taps[:, :inner] = conv_value[...].astype(f32) * 0.5
        taps[:, inner:] = conv_state[...].astype(f32) * 0.5
        rate[...] = jnp.zeros_like(rate)
        rate[:, :heads] = jnp.exp(decay_log[...])
        pick[...] = picks(0, inner)

    total = jnp.zeros((1, LANES), f32)
    for c in range(blocks):
        part = running_sum(-steps[pl.ds(c * BLOCK, BLOCK), :] * rate[...]) + total
        sums[pl.ds(c * BLOCK, BLOCK), :] = part
        total = part[BLOCK - 1 : BLOCK]

    last_start = start_at(starts, first + rows - 1)
    first_end = start_after(starts, first)

    end_state = jnp.zeros((STATE, inner), f32)
    begin_state = jnp.zeros((STATE, inner), f32)
    for c in range(blocks):
        at = pl.ds(c * BLOCK, BLOCK)
        tile_up(win, pl.ds(HALO, BLOCK), mix[at, :].astype(f32))
        if c == 0:
            ahead = jnp.where(quarter == 0, edge[:HALO], before[...].astype(f32))
        else:
            ahead = mix[c * BLOCK - HALO : c * BLOCK, :].astype(f32)
        if c == blocks - 1:
            behind = jnp.where(quarter == quarters - 1, edge[HALO:], after[...].astype(f32))
        else:
            behind = mix[(c + 1) * BLOCK : (c + 1) * BLOCK + HALO, :].astype(f32)

        tile_up(win, pl.ds(0, HALO), ahead)
        tile_up(win, pl.ds(HALO + BLOCK, HALO), behind)

        def put(tile, at, forward, backward):
            xf[tile, at, :] = forward
            xb[tile, at, :] = backward

        here = first + c * BLOCK
        convolve_block(win, 0, taps, starts, here, put)
        dt = steps[at, :]
        inclusive = sums[at, :]
        weight_f = dt * jnp.exp(total - inclusive)
        weight_b = dt * jnp.exp(inclusive + dt * rate[...])
        position = iota((BLOCK, 1), 0) + here
        spread_f = dot(halves_of(weight_f), pick[...])
        spread_b = dot(halves_of(weight_b), pick[...])
        write_f = jnp.where(position >= last_start, xf[value_tiles, :BLOCK], 0.0).astype(bf16)
        write_b = jnp.where(position < first_end, xb[value_tiles, :BLOCK], 0.0).astype(bf16)
        end_state += dot_first(write_f, (side_by_side(xf.at[:value_tiles]) * spread_f).astype(bf16))
        begin_state += dot_first(write_b, (side_by_side(xb.at[:value_tiles]) * spread_b).astype(bf16))

    ends[0] = end_state
    begins[0] = begin_state
    decay = dot(halves_of(jnp.broadcast_to(jnp.exp(total), (SUB, LANES))), pick[...])
    pass_f = jnp.where(last_start < first, decay, 0.0)
    pass_b = jnp.where(first_end > first + rows, decay, 0.0)
    passes[0, :8] = pass_f
    passes[0, 8:] = pass_b
    through_f = total_f[STATE : STATE + 1]
    through_b = total_b[STATE : STATE + 1]
    total_f[:STATE] = pass_f[:1] * total_f[:STATE] + end_state
    total_b[:STATE] = total_b[:STATE] + through_b * begin_state
    total_f[STATE : STATE + 1] = through_f * pass_f[:1]
    total_b[STATE : STATE + 1] = through_b * pass_b[:1]

    @pl.when(quarter == quarters - 1)
    def _():
        place = info[1]
        for total_ref, later in ((total_f, True), (total_b, False)):
            state = total_ref[:STATE].astype(bf16)
            high, low = split_halves(total_ref[STATE : STATE + 1])
            pad = jnp.zeros((HALO - 2, inner), f32)
            extra = jnp.concatenate([high.astype(f32), low.astype(f32), pad], axis=0).astype(bf16)

            def fill(p, carry):
                @pl.when((p > place) if later else (p <= place))
                def _():
                    sent[p, :STATE] = state
                    sent[p, STATE:] = extra

                return carry

            lax.fori_loop(0, places, fill, 0)


def carry_kernel(places, quarters, info, got, ends, begins, passes, out):
    place = info[1]
    shape = ends.shape[1:]

    def step(p, state):
        decay = got[p, STATE : STATE + HALO].astype(f32)
        return (decay[0:1] + decay[1:2]) * state + got[p, :STATE].astype(f32)

    def forward(p, state):
        return step(p, state)

    def backward(p, state):
        return step(places - 1 - p, state)

    state = lax.fori_loop(0, place, forward, jnp.zeros(shape, f32))
    for q in range(quarters):
        out[q, 0] = state.astype(bf16)
        state = passes[q, 0:1] * state + ends[q]
    state = lax.fori_loop(0, places - 1 - place, backward, jnp.zeros(shape, f32))
    for q in reversed(range(quarters)):
        out[q, 1] = state.astype(bf16)
        state = passes[q, 8:9] * state + begins[q]


def shared_kernel(
    groups,
    group_heads,
    pieces,
    lengths,
    info,
    hidden,
    above,
    below,
    halo_before,
    halo_after,
    gain,
    state_w,
    conv_state,
    *refs,
):
    smalls, refs = refs[:groups], refs[groups:]
    (
        normed_out,
        factors,
        reach,
        raw,
        raw_t,
        mix_f,
        mix_b,
        write_f,
        write_b,
        read_f,
        read_b,
        enter_f,
        enter_b,
        flags,
        wide,
        xf,
        xb,
        taps,
        step_w,
    ) = refs
    heads = groups * group_heads
    kinds = LANES // heads
    rows = hidden.shape[0]
    blocks = rows // BLOCK
    me = info[3]
    first = info[2]
    starts = bounds_of(lengths, pieces)
    taps[...] = conv_state[...].astype(f32) * 0.5
    for k in range(kinds):
        for g in range(groups):
            at = k * heads + g * group_heads
            step_w[at : at + group_heads, :] = smalls[g][:group_heads, :]
    bias = jnp.zeros((1, LANES), f32)
    rate = jnp.zeros((1, LANES), f32)
    own_lane = iota((1, LANES), 1) < group_heads
    for g in range(groups):
        at = group_heads + CONV + 2
        one_bias = jnp.where(own_lane, smalls[g][at : at + 1, :LANES], 0.0)
        one_rate = jnp.where(own_lane, jnp.exp(smalls[g][at + 1 : at + 2, :LANES]), 0.0)
        for k in range(kinds):
            shift = k * heads + g * group_heads
            bias += pltpu.roll(one_bias, shift, 1) if shift else one_bias
            rate += pltpu.roll(one_rate, shift, 1) if shift else one_rate
    wide_gain = gain[...].astype(f32)
    normed_out[HALO : HALO + rows, :] = normalise(hidden[...], wide_gain)
    ahead = jnp.where(me == 0, halo_before[...].astype(f32), above[...].astype(f32))
    normed_out[:HALO, :] = normalise(ahead, wide_gain)
    behind = jnp.where(me == groups - 1, halo_after[...].astype(f32), below[...].astype(f32))
    normed_out[HALO + rows :, :] = normalise(behind, wide_gain)
    all_steps = dot_last(normed_out[HALO : HALO + rows, :], step_w[...].astype(bf16))
    tile_up(wide, slice(None), dot(normed_out[...], state_w[...]).astype(bf16).astype(f32))
    kind = lax.div(iota((1, LANES), 1), heads)
    totals = []
    for c in range(blocks):
        at = pl.ds(c * BLOCK, BLOCK)
        dt = softplus(all_steps[c * BLOCK : (c + 1) * BLOCK] + bias)
        log_step = -dt * rate
        upto = running_sum(log_step)
        total = upto[BLOCK - 1 : BLOCK]
        onward = total - upto + log_step
        totals.append(total)
        flags[c] = jnp.where(jnp.max(-total) > SAFE, 1, 0)
        value = jnp.where(kind == 0, upto, jnp.where(kind == 1, dt, jnp.where(kind == 2, onward, total)))
        raw[at, :] = value
        raw_t[c] = jnp.transpose(value)
        power = jnp.where(
            kind == 0, upto, jnp.where(kind == 1, -upto, jnp.where(kind == 2, onward, -onward))
        )
        factor = jnp.exp(jnp.minimum(power, SAFE)) * jnp.where((kind & 1) == 1, dt, 1.0)
        factors[at, :] = halves_of(factor)

    zero = jnp.zeros((1, LANES), f32)
    ahead = [zero]
    for c in range(blocks - 1):
        ahead.append(ahead[-1] + totals[c])
    behind = [zero]
    for c in reversed(range(1, blocks)):
        behind.insert(0, behind[0] + totals[c])
    quarter_end = start_after(starts, first - 1)
    quarter_start = start_at(starts, first + rows)
    for c in range(blocks):
        at = pl.ds(c * BLOCK, BLOCK)
        value = raw[at, :]
        power = jnp.where(kind == 0, value + ahead[c], value + behind[c])
        factor = jnp.where((kind & 1) == 0, jnp.exp(jnp.minimum(power, 0.0)), 0.0)
        reach[at, :] = halves_of(factor)

        here = first + c * BLOCK

        def put(tile, at, forward, backward):
            xf[tile, at, :] = forward
            xb[tile, at, :] = backward

        convolve_block(wide, c * BLOCK, taps, starts, here, put)
        position = iota((BLOCK, 1), 0) + here
        begin, end = piece_bounds(starts, position)
        other = iota((BLOCK, BLOCK), 1) + here
        for x, mix, write, read, enter, ahead_of in (
            (xf, mix_f, write_f, read_f, enter_f, True),
            (xb, mix_b, write_b, read_b, enter_b, False),
        ):
            writes = x[0, :BLOCK]
            reads = x[1, :BLOCK]
            inner_product = dot_last(reads.astype(bf16), writes.astype(bf16))
            if ahead_of:
                allowed = (other <= position) & (other >= begin)
                keep = position >= start_at(starts, here + BLOCK - 1)
                opened = position < start_after(starts, here - 1)
                entered = position < quarter_end
            else:
                allowed = (other >= position) & (other < end)
                keep = position < start_after(starts, here)
                opened = position >= start_at(starts, here + BLOCK)
                entered = position >= quarter_start
            mix[c] = jnp.where(allowed, inner_product, 0.0).astype(bf16)
            write[at, :] = jnp.where(keep, writes, 0.0).astype(bf16)
            read[at, :] = jnp.where(opened, reads, 0.0).astype(bf16)
            enter[at, :] = jnp.where(entered, reads, 0.0).astype(bf16)


def group_kernel(
    group,
    split,
    group_heads,
    heads,
    pieces,
    lengths,
    info,
    flags,
    normed,
    factors,
    raw,
    raw_t,
    mix_f,
    mix_b,
    write_f,
    write_b,
    read_f,
    read_b,
    *refs,
):
    members = len(split)
    count = sum(sum(pair) for pair in split)
    smalls, weights, refs = refs[:members], refs[members : members + count], refs[members + count :]
    out_f, out_b, gate_out, held, sems, win, xf, xb, acc, state_f, state_b, pick, taps, skip = refs
    step = pl.program_id(0)
    copies, owners, at = [], [], 0
    for k, pair in enumerate(split):
        for which, number in enumerate(pair):
            row = 0
            for _ in range(number):
                size = weights[at].shape[0]
                target = held.at[2 * k + which, row : row + size]
                copies.append(pltpu.make_async_copy(weights[at], target, sems.at[at]))
                owners.append(k)
                row += size
                at += 1

    @pl.when(step == 0)
    def _():
        for copy in copies:
            copy.start()

    out_f, out_b, gate_out = (r.at[0] for r in (out_f, out_b, gate_out))
    value_w, gate_w = held.at[2 * step], held.at[2 * step + 1]
    inner = held.shape[2]
    rows = out_f.shape[0]
    blocks = rows // BLOCK
    first = info[2]
    starts = bounds_of(lengths, pieces)
    offset = (step + group) * group_heads
    for kind in range(pick.shape[0]):
        pick[kind] = picks(kind * heads + offset, inner)
    for k in range(members):

        @pl.when(step == k)
        def _():
            taps[...] = smalls[k][group_heads : group_heads + CONV, :inner] * 0.5
            skip[...] = smalls[k][group_heads + CONV + 1 : group_heads + CONV + 2, :inner]
            for copy, owner in zip(copies, owners):
                if owner == k:
                    copy.wait()

    tile_up(win, slice(None), dot(normed[...], value_w[...]).astype(bf16).astype(f32))

    def prepare(c, unused):
        at = pl.ds(pl.multiple_of(c * BLOCK, BLOCK), BLOCK)
        centre = normed[pl.ds(pl.multiple_of(c * BLOCK, BLOCK) + HALO, BLOCK), :]
        gate = dot(centre, gate_w[...]).astype(bf16).astype(f32) * 0.5
        gate_out[at, :] = (gate * jnp.tanh(gate) + gate).astype(bf16)

        def put(tile, at, forward, backward):
            xf[c, tile, at, :] = forward
            xb[c, tile, at, :] = backward

        convolve_block(win, c * BLOCK, taps, starts, first + c * BLOCK, put)
        return unused

    lax.fori_loop(0, blocks, prepare, 0)
    state_f[0] = jnp.zeros(state_f.shape[1:], f32)
    state_b[0] = jnp.zeros(state_b.shape[1:], f32)

    ways = (
        (xf, mix_f, write_f, read_f, out_f, state_f, 0, BLOCK - 1),
        (xb, mix_b, write_b, read_b, out_b, state_b, 2, 0),
    )

    def quick(way, c, now, passing):
        x, mix, write, read, out, state, kind, edge_row = way
        at = pl.ds(pl.multiple_of(c * BLOCK, BLOCK), BLOCK)
        here_factors = factors[at, :]
        grow = dot(here_factors, pick[kind])
        carried = state[now]
        values = side_by_side(x.at[c])
        scaled = (values * dot(here_factors, pick[kind + 1])).astype(bf16)
        total = dot(mix[c], scaled) + dot(read[at, :], carried.astype(bf16))
        out[at, :] = (total * grow + skip[...] * values).astype(bf16)
        through = jnp.where(passing, 1.0, 0.0)
        fresh = dot_first(write[at, :], scaled)
        state[1 - now] = grow[edge_row : edge_row + 1] * (fresh + through * carried)

    def general(way, c, now, passing):
        x, mix, write, read, out, state, kind, edge_row = way
        at = pl.ds(pl.multiple_of(c * BLOCK, BLOCK), BLOCK)
        grow = dot(factors[at, :], pick[kind])
        carried = state[now]
        pairs = mix[c].astype(f32)
        lane = iota((1, LANES), 1)
        half = lane >= HEAD_DIM
        values = raw[at, :]

        def pair(p, unused):
            cols = pl.ds(pl.multiple_of(p * LANES, LANES), LANES)
            x_pair = x[c, p, :BLOCK].astype(bf16)
            sums = []
            for side in range(LANES // HEAD_DIM):
                head = offset + p * (LANES // HEAD_DIM) + side
                down = jnp.sum(jnp.where(lane == head + kind * heads, values, 0.0), axis=1, keepdims=True)
                across = raw_t[c, pl.ds(head + kind * heads, 1), :]
                head_steps = raw_t[c, pl.ds(head + heads, 1), :]
                table = pairs * jnp.exp(jnp.minimum(down - across, 0.0)) * head_steps
                sums.append(dot(table.astype(bf16), x_pair))
            acc[:, cols] = jnp.where(half, sums[1], sums[0])
            return unused

        lax.fori_loop(0, inner // LANES, pair, 0)
        wide = side_by_side(x.at[c])
        from_state = dot(read[at, :], carried.astype(bf16))
        out[at, :] = (acc[...] + grow * from_state + skip[...] * wide).astype(bf16)
        head_steps = pltpu.roll(values, (kind - 1) * heads % LANES, 1)
        gap = jnp.minimum(values[edge_row : edge_row + 1] - values, 0.0)
        weight = jnp.where(lax.div(lane, heads) == kind, head_steps * jnp.exp(gap), 0.0)
        scaled = (wide * dot(halves_of(weight), pick[kind])).astype(bf16)
        through = jnp.where(passing, 1.0, 0.0)
        decay = grow[edge_row : edge_row + 1]
        state[1 - now] = dot_first(write[at, :], scaled) + through * decay * carried

    def both(k, unused):
        now = k & 1
        spots = []
        for way, c in zip(ways, (k, blocks - 1 - k)):
            here = first + c * BLOCK
            if way is ways[0]:
                passing = start_at(starts, here + BLOCK - 1) < here
            else:
                passing = start_after(starts, here) > here + BLOCK
            spots.append((way, c, now, passing))
        for spot in spots:
            quick(*spot)
        for spot in spots:

            @pl.when(flags[spot[1]] != 0)
            def _():
                general(*spot)

        return unused

    lax.fori_loop(0, blocks, both, 0)


def finish_kernel(split, group_heads, heads, info, *refs):
    groups = len(split)
    hidden, reach, enter_f, enter_b, carries = refs[:5]
    gains, refs = refs[5 : 5 + groups], refs[5 + groups :]
    gain_row = group_heads + CONV
    tile = hidden.shape[0]
    out_f, out_b, gates = (refs[k * groups : (k + 1) * groups] for k in range(3))
    weights = refs[3 * groups : 3 * groups + sum(split)]
    out, held_f, held_b = refs[3 * groups + sum(split) :]
    me = info[3]
    inner = out_f[0].shape[2]
    here_reach = reach[...]
    sums = [jnp.zeros((tile, 1), f32), jnp.zeros((tile, 1), f32)]
    for g in range(groups):
        gate = gates[g][0].astype(f32)
        for k, (base, enter, held) in enumerate(((out_f, enter_f, held_f), (out_b, enter_b, held_b))):
            grow = dot(here_reach, picks(2 * k * heads + g * group_heads, inner))
            full = base[g][0].astype(f32) + grow * dot(enter[...], carries[me ^ g, k])
            gated = full * gate
            held[:, g * inner : (g + 1) * inner] = gated
            sums[k] = sums[k] + jnp.sum(gated * gated, axis=1, keepdims=True)
    scale_f, scale_b = (lax.rsqrt(s / (groups * inner) + EPSILON) for s in sums)
    total = hidden[...].astype(f32)
    for g in range(groups):
        cols = slice(g * inner, (g + 1) * inner)
        combined = (held_f[:, cols] * scale_f + held_b[:, cols] * scale_b) * gains[g][gain_row : gain_row + 1, :inner]
        combined = combined.astype(bf16)
        row = 0
        for weight in weights[sum(split[:g]) : sum(split[: g + 1])]:
            size = weight.shape[0]
            total = total + dot(combined[:, row : row + size], weight[...])
            row += size
    out[...] = total.astype(bf16)


def whole(shape):
    return pl.BlockSpec(shape, lambda *_: (0,) * len(shape))


def struct(shape, dtype):
    return jax.ShapeDtypeStruct(shape, dtype)


def call(kernel, grid, scalars, arrays, in_specs, out_shape, out_specs, scratch, name):
    return pl.pallas_call(
        kernel,
        grid_spec=pltpu.PrefetchScalarGridSpec(
            num_scalar_prefetch=len(scalars),
            grid=grid,
            in_specs=in_specs,
            out_specs=out_specs,
            scratch_shapes=scratch,
        ),
        out_shape=out_shape,
        compiler_params=pltpu.CompilerParams(
            dimension_semantics=("arbitrary",) * len(grid), vmem_limit_bytes=VMEM_LIMIT
        ),
        name=name,
    )(*scalars, *arrays)


def swap(x, axis, distance):
    return lax.ppermute(x, axis, [(i, i ^ distance) for i in range(lax.axis_size(axis))])


def from_far(x, groups):
    return {k: swap(x, "head", k) for k in range(2, groups, 2)}


def gather_near(x, far, groups):
    held = [[x]] + [None] * (groups - 1)
    for k in range(2, groups, 2):
        held[k] = [part[k] for part in far]
    for k in range(1, groups, 2):
        held[k] = [swap(part, "head", 1) for part in held[k - 1]]
    return held


def cut_rows(x):
    middle = x.shape[0] // 2
    return x[:middle], x[middle:]


def local(
    hidden_in,
    norm_gain,
    gate_weight,
    value_weight,
    state_weight,
    step_weight,
    step_bias,
    decay_log,
    skip_gain,
    conv_value,
    conv_state,
    output_gain,
    output_weight,
    piece_lengths,
):
    tokens, width = hidden_in.shape
    group_heads = step_bias.shape[0]
    inner = value_weight.shape[1]
    groups = lax.axis_size("head")
    places = lax.axis_size("seq")
    heads = group_heads * groups
    me = lax.axis_index("head")
    place = lax.axis_index("seq")
    rows = tokens // groups
    blocks = rows // BLOCK
    pieces = piece_lengths.shape[0]

    up = [(i, i + 1) for i in range(places - 1)]
    down = [(i + 1, i) for i in range(places - 1)]
    before = lax.ppermute(hidden_in[-HALO:], "seq", up)
    after = lax.ppermute(hidden_in[:HALO], "seq", down)
    small = [step_weight.T, conv_value, output_gain.reshape(1, -1)]
    small += [jnp.repeat(skip_gain, HEAD_DIM).reshape(1, -1), step_bias.reshape(1, -1)]
    small += [decay_log.reshape(1, -1)]
    small = jnp.concatenate(
        [jnp.pad(a.astype(f32), ((0, 0), (0, width - a.shape[1]))) for a in small], axis=0
    )
    far_smalls = from_far(small, groups)
    value_first, value_second = cut_rows(value_weight)
    far_first = from_far(value_first, groups)
    info = jnp.stack([place * tokens, place, place * tokens + me * rows, me]).astype(jnp.int32)
    gain = norm_gain.reshape(1, width)

    tile = min(1024, rows)
    columns = inner + STATE
    mix, steps = call(
        functools.partial(project_kernel, inner, group_heads),
        (tokens // tile,),
        (),
        (hidden_in, gain, value_weight, state_weight, step_weight.T, step_bias.reshape(1, -1)),
        [
            pl.BlockSpec((tile, width), lambda i: (i, 0)),
            whole((1, width)),
            whole((width, inner)),
            whole((width, STATE)),
            whole((group_heads, width)),
            whole((1, group_heads)),
        ],
        [struct((tokens, columns), bf16), struct((tokens, LANES), f32)],
        [pl.BlockSpec((tile, columns), lambda i: (i, 0)), pl.BlockSpec((tile, LANES), lambda i: (i, 0))],
        [pltpu.VMEM((width, columns + LANES), bf16), pltpu.VMEM((1, LANES), f32)],
        "project",
    )
    before, after, far_smalls, far_first, value_second, mix = lax.optimization_barrier(
        (before, after, far_smalls, far_first, value_second, mix)
    )
    far_second = from_far(value_second, groups)
    per = rows // HALO
    state_shape = (groups, STATE, inner)
    one_state = pl.BlockSpec((1, STATE, inner), lambda i, *_: (i, 0, 0))
    ends, begins, passes, sent = call(
        functools.partial(state_kernel, inner, group_heads, pieces, places),
        (groups,),
        (piece_lengths, info),
        (
            mix,
            mix,
            mix,
            before,
            after,
            gain,
            value_weight,
            state_weight,
            steps,
            decay_log.reshape(1, -1),
            conv_value,
            conv_state,
        ),
        [
            pl.BlockSpec((rows, columns), lambda i, *_: (i, 0)),
            pl.BlockSpec((HALO, columns), lambda i, *_: (jnp.maximum(i * per - 1, 0), 0)),
            pl.BlockSpec(
                (HALO, columns), lambda i, *_: (jnp.minimum((i + 1) * per, tokens // HALO - 1), 0)
            ),
            whole((HALO, width)),
            whole((HALO, width)),
            whole((1, width)),
            whole((width, inner)),
            whole((width, STATE)),
            pl.BlockSpec((rows, LANES), lambda i, *_: (i, 0)),
            whole((1, group_heads)),
            whole((CONV, inner)),
            whole((CONV, STATE)),
        ],
        [
            struct(state_shape, f32),
            struct(state_shape, f32),
            struct((groups, 2 * SUB, inner), f32),
            struct((places, STATE + HALO, inner), bf16),
        ],
        [
            one_state,
            one_state,
            pl.BlockSpec((1, 2 * SUB, inner), lambda i, *_: (i, 0, 0)),
            whole((places, STATE + HALO, inner)),
        ],
        [
            pltpu.VMEM((2 * HALO, columns), f32),
            pltpu.VMEM((columns // LANES, WINDOW, LANES), f32),
            pltpu.VMEM((columns // LANES, COVER, LANES), f32),
            pltpu.VMEM((columns // LANES, COVER, LANES), f32),
            pltpu.VMEM((rows, LANES), f32),
            pltpu.VMEM((STATE + SUB, inner), f32),
            pltpu.VMEM((STATE + SUB, inner), f32),
            pltpu.VMEM((CONV, columns), f32),
            pltpu.VMEM((1, LANES), f32),
            pltpu.VMEM((2 * LANES, inner), bf16),
        ],
        "states",
    )

    far_second, sent, gate_weight, output_weight = lax.optimization_barrier(
        (far_second, sent, gate_weight, output_weight)
    )
    values = gather_near(value_weight, [far_first, far_second], groups)
    smalls = [piece[0] for piece in gather_near(small, [far_smalls], groups)]
    far_gates = from_far(gate_weight, groups)
    out_first, out_second = cut_rows(output_weight)
    far_out_first = from_far(out_first, groups)
    got = lax.all_to_all(sent, "seq", split_axis=0, concat_axis=0, tiled=True)

    near_shape = (rows + 2 * HALO, width)
    square = struct((blocks, BLOCK, BLOCK), bf16)
    thin = struct((rows, STATE), bf16)
    shapes = [
        struct(near_shape, bf16),
        struct((rows, 2 * LANES), bf16),
        struct((rows, 2 * LANES), bf16),
        struct((rows, LANES), f32),
        struct((blocks, LANES, BLOCK), f32),
        square,
        square,
        thin,
        thin,
        thin,
        thin,
        thin,
        thin,
        struct((blocks,), jnp.int32),
    ]
    shared = call(
        functools.partial(shared_kernel, groups, group_heads, pieces),
        (1,),
        (piece_lengths, info),
        (hidden_in, hidden_in, hidden_in, before, after, gain, state_weight, conv_state, *smalls),
        [
            pl.BlockSpec((rows, width), lambda i, l, at: (at[3], 0)),
            pl.BlockSpec((HALO, width), lambda i, l, at: (jnp.maximum(at[3] * per - 1, 0), 0)),
            pl.BlockSpec(
                (HALO, width), lambda i, l, at: (jnp.minimum((at[3] + 1) * per, tokens // HALO - 1), 0)
            ),
            whole((HALO, width)),
            whole((HALO, width)),
            whole((1, width)),
            whole((width, 2 * STATE)),
            whole((CONV, 2 * STATE)),
        ]
        + [whole(small.shape)] * groups,
        shapes,
        [whole(s.shape) for s in shapes[:-1]] + [pl.BlockSpec(memory_space=pltpu.SMEM)],
        [
            pltpu.VMEM((2, rows + 2 * HALO, STATE), f32),
            pltpu.VMEM((2, COVER, STATE), f32),
            pltpu.VMEM((2, COVER, STATE), f32),
            pltpu.VMEM((CONV, 2 * STATE), f32),
            pltpu.VMEM((LANES, width), f32),
        ],
        "shared",
    )
    normed, factors, reach, raw, raw_t, mix_f, mix_b, write_f, write_b, read_f, read_b = shared[:11]
    enter_f, enter_b, flags = shared[11:]
    members = min(2, groups)
    done = []

    def do_groups(g):
        arrays = (normed, factors, raw, raw_t, mix_f, mix_b, write_f, write_b, read_f, read_b)
        arrays += tuple(smalls[g : g + members])
        loaded = [values[k] + gates[k] for k in range(g, g + members)]
        split = [(len(values[k]), len(gates[k])) for k in range(g, g + members)]
        loaded = [w for ws in loaded for w in ws]
        done.append(
            call(
                functools.partial(group_kernel, g, split, group_heads, heads, pieces),
                (members,),
                (piece_lengths, info, flags),
                arrays + tuple(loaded),
                [whole(a.shape) for a in arrays] + [pl.BlockSpec(memory_space=pl.ANY)] * len(loaded),
                [struct((members, rows, inner), bf16)] * 3,
                [pl.BlockSpec((1, rows, inner), lambda i, *_: (i, 0, 0))] * 3,
                [
                    pltpu.VMEM((2 * members, width, inner), bf16),
                    pltpu.SemaphoreType.DMA((len(loaded),)),
                    pltpu.VMEM((inner // LANES, rows + 2 * HALO, LANES), f32),
                    pltpu.VMEM((blocks, inner // LANES, COVER, LANES), f32),
                    pltpu.VMEM((blocks, inner // LANES, COVER, LANES), f32),
                    pltpu.VMEM((BLOCK, inner), f32),
                    pltpu.VMEM((2, STATE, inner), f32),
                    pltpu.VMEM((2, STATE, inner), f32),
                    pltpu.VMEM((LANES // heads, 2 * LANES, inner), bf16),
                    pltpu.VMEM((CONV, inner), f32),
                    pltpu.VMEM((1, inner), f32),
                ],
                "group%d" % g,
            )
        )

    gates = [[gate_weight], [swap(gate_weight, "head", 1)]][:groups]
    do_groups(0)
    got, done[0], far_out_first, far_gates, out_second = lax.optimization_barrier(
        (got, done[0], far_out_first, far_gates, out_second)
    )
    gates += gather_near(gate_weight, [far_gates], groups)[members:]
    far_out_second = from_far(out_second, groups)
    entering = call(
        functools.partial(carry_kernel, places, groups),
        (1,),
        (info,),
        (got, ends, begins, passes),
        [whole(a.shape) for a in (got, ends, begins, passes)],
        struct((groups, 2, STATE, inner), bf16),
        whole((groups, 2, STATE, inner)),
        [],
        "carries",
    )
    carries = lax.all_to_all(entering, "head", split_axis=0, concat_axis=0, tiled=True)

    for g in range(members, groups, members):
        do_groups(g)
    outs = gather_near(output_weight, [far_out_first, far_out_second], groups)

    tile = min(512, rows)
    tiles = rows // tile

    def by_tile(columns):
        return pl.BlockSpec((tile, columns), lambda i, _: (i, 0))

    def member(k):
        return pl.BlockSpec((1, tile, inner), lambda i, _: (k, i, 0))

    members_of = [(done[g // members], g % members) for g in range(groups)]
    return call(
        functools.partial(finish_kernel, [len(pieces_of) for pieces_of in outs], group_heads, heads),
        (tiles,),
        (info,),
        (hidden_in, reach, enter_f, enter_b, carries, *smalls)
        + tuple(arrays[k] for k in range(3) for arrays, _ in members_of)
        + tuple(piece for pieces_of in outs for piece in pieces_of),
        [
            pl.BlockSpec((tile, width), lambda i, at: (at[3] * tiles + i, 0)),
            by_tile(2 * LANES),
            by_tile(STATE),
            by_tile(STATE),
            whole(carries.shape),
        ]
        + [whole(small.shape)] * groups
        + [member(k) for _, k in members_of] * 3
        + [whole(piece.shape) for pieces_of in outs for piece in pieces_of],
        struct((rows, width), bf16),
        by_tile(width),
        [pltpu.VMEM((tile, groups * inner), f32), pltpu.VMEM((tile, groups * inner), f32)],
        "finish",
    )


def solution(mesh):
    in_specs = (
        P("seq", None),
        P(),
        P(None, "head"),
        P(None, "head"),
        P(),
        P(None, "head"),
        P("head"),
        P("head"),
        P("head"),
        P(None, "head"),
        P(),
        P("head"),
        P("head", None),
        P(),
    )
    out_specs = P(("seq", "head"), None)
    return jax.shard_map(local, mesh=mesh, in_specs=in_specs, out_specs=out_specs, check_vma=False)
```

time: 244 us -> 166 us (0.68); the launches traced: 239 us -> 164 us
  Pallas kernels: 145 us -> 117 us
  local copies, waits for them, and re-layouts: 25.3 us -> 9.47 us
  between operations: 14.6 us -> 0.58 us
  waiting for transfers between devices: 19.4 us -> 8.98 us
  other arithmetic: 7.31 us -> 0.69 us
    pallas_call x9 -> x7, Pallas kernels: 145 us -> 117 us  [call(): pl.pallas_call(kernel, grid_spec=pltpu.PrefetchScalarGridSpec(num_scalar_...]
    all_to_all x1, waiting for transfers between devices: 19.4 us -> 0.01 us  [local(): got = lax.all_to_all(sent, 'seq', split_axis=0, concat_axis=0, tiled=True)]
    ppermute x9 -> x16, waiting for transfers between devices: 0.02 us -> 8.97 us  [swap(): lax.ppermute(x, axis, [(i, i ^ distance) for i in range(lax.axis_size(axi...]
    all_to_all x1, starting transfers between devices: 13.2 us -> 8.03 us  [local(): got = lax.all_to_all(sent, 'seq', split_axis=0, concat_axis=0, tiled=True)]
    ppermute x9 -> x16, starting transfers between devices: 6.15 us -> 10.2 us  [swap(): lax.ppermute(x, axis, [(i, i ^ distance) for i in range(lax.axis_size(axi...]
    broadcast_in_dim x8 -> x1, local copies, waits for them, and re-layouts: 2.94 us -> 0.07 us  [local(): jnp.repeat(skip_gain, HEAD_DIM).reshape(1, -1)]
    unnamed x25 -> x46, local copies, waits for them, and re-layouts: 5.11 us -> 5.69 us
  transfers between devices with their start and end apart: 14 -> 20, of which waited for: 1 -> 3; matrix products, arithmetic and copies ran while one was open for 12% -> 2% of each run, Pallas kernels for 54% -> 61%
where the time goes in v1:
time: 166 us; the launch traced here: 164 us
  Pallas kernels  117 us (70%)
  starting transfers between devices  27.1 us (16%)
  local copies, waits for them, and re-layouts  9.47 us (6%)
  waiting for transfers between devices  8.98 us (5%)
    pallas_call x7, Pallas kernels, call(): pl.pallas_call(kernel, grid_spec=pltpu.PrefetchScalarGridSpec(num_scalar_...  117 us
    ppermute x16, starting transfers between devices, swap(): lax.ppermute(x, axis, [(i, i ^ distance) for i in range(lax.axis_size(axi...  10.2 us
    ppermute x16, waiting for transfers between devices, swap(): lax.ppermute(x, axis, [(i, i ^ distance) for i in range(lax.axis_size(axi...  8.97 us
    all_to_all x1, starting transfers between devices, local(): got = lax.all_to_all(sent, 'seq', split_axis=0, concat_axis=0, tiled=True)  8.03 us
    unnamed x46, local copies, waits for them, and re-layouts  5.69 us
    ppermute x1, starting transfers between devices, local(): before = lax.ppermute(hidden_in[-HALO:], 'seq', up)  3.86 us
    all_to_all x1, starting transfers between devices, local(): lax.all_to_all(entering, 'head', split_axis=0, concat_axis=0, tiled=True)  3.78 us
  transfers between devices with their start and end apart: 20, of which 3 were waited for; matrix products, arithmetic and copies ran while one was open for 2% of the time, Pallas kernels for 61%

profile of v1, /device:TPU:0, one launch (start us, length us, event | category | flops | bytes accessed | tf_op | source)
XLA Modules:
  0.0 164.2 jit_solution(915618031447694629)
XLA Ops:
  0.0 1.3 fusion.2
  1.4 3.0 %collective-permute-start.3 = (bf16[512,512]{1,0:T(8,128)(2,1)S(1)}, bf16[512,512]{1,0:T(8,128)(2,1)}, u32[]{:S(2)}, u32[]{:S(2)}) collective-permute-start(bf16[512,512]{1,0:T(8,128)(2,1)S(1)} %get-tuple-element.96), channel_id=1, source_target_pairs={{0,2},{1,3},{2,0},{3,1},{4,6},{5,7},{6,4},{7,5},{8,10},{9,11},{10,... | collective-permute-start | bytes 1572872 | tf_op jit(solution)/shard_map/ppermute | solution.py:696
  5.6 3.9 %collective-permute-start = (bf16[16,1024]{1,0:T(8,128)(2,1)S(1)}, bf16[16,1024]{1,0:T(8,128)(2,1)S(1)}, u32[]{:S(2)}, u32[]{:S(2)}) collective-permute-start(bf16[16,1024]{1,0:T(8,128)(2,1)S(1)} %get-tuple-element.92), channel_id=1, source_target_pairs={{0,4},{4,8},{8,12},{12,16},{16,20},{20,24},{24,28},{1,5},{5,9},{9,... | collective-permute-start | bytes 98312 | tf_op jit(solution)/shard_map/ppermute | solution.py:747
  9.5 1.3 collective-permute-start.1
  11.4 12.2 %project.1 = (bf16[4096,640]{1,0:T(8,128)(2,1)}, f32[4096,128]{1,0:T(8,128)}) custom-call(bf16[4096,1024]{1,0:T(8,128)(2,1)} %refs_0_.1, bf16[1,1024]{1,0:T(2,128)(2,1)} %reshape.16.gain, bf16[1024,512]{1,0:T(8,128)(2,1)} %refs_2_.1, bf16[1024,256]{1,0:T(8,128)(2,1)} %state_w.5, bf16[8,1024]{1,0:T(8,128)(2,1)} %bitcast.8, f32[1,8]{1,0:T(1,128)} %bitcast.9), custom_call_target="tpu_custom_call" | custom-call | tf_op jit(solution)/shard_map/project/pallas_call | solution.py:678
  23.7 1.6 collective-permute-start.6
  25.9 22.5 %states.1 = (f32[4,128,512]{2,1,0:T(8,128)}, f32[4,128,512]{2,1,0:T(8,128)}, f32[4,16,512]{2,1,0:T(8,128)}, bf16[8,144,512]{2,1,0:T(8,128)(2,1)}) custom-call(s32[16]{0:T(128)} %lengths.7, s32[4]{0:T(128)} %pad_add_fusion.info, bf16[4096,640]{1,0:T(8,128)(2,1)} %get-tuple-element.56.mix.before.after, bf16[4096,640]{1,0:T(8,128)(2,1)} %get-tuple-element.56.mix.before.after, ...), custom_call_target="tpu_custom_call" | custom-call | tf_op jit(solution)/shard_map/states/pallas_call | solution.py:678
  48.5 0.8 copy-done.12
  49.3 8.0 %all-to-all-start = ((bf16[8,144,512]{2,1,0:T(8,128)(2,1)}), bf16[8,144,512]{2,1,0:T(8,128)(2,1)S(1)}, u32[]{:S(2)}, u32[]{:S(2)}) async-start(bf16[8,144,512]{2,1,0:T(8,128)(2,1)} %get-tuple-element.59), calls=%async_computation | async-start | bytes 2359296 | tf_op jit(solution)/shard_map/all_to_all | solution.py:857
  58.4 0.8 fusion.1
  59.3 1.5 collective-permute-start.9
  60.8 1.3 collective-permute-done.4.refs_1_.refs_6_
  62.2 1.1 collective-permute-done.5.refs_3_.refs_1_.refs_8_
  63.9 11.4 %shared.1 = (bf16[1056,1024]{1,0:T(8,128)(2,1)}, bf16[1024,256]{1,0:T(8,128)(2,1)}, bf16[1024,256]{1,0:T(8,128)(2,1)}, f32[1024,128]{1,0:T(8,128)}, f32[4,128,25...) custom-call(s32[16]{0:T(128)} %lengths.7, ...), custom_call_target="tpu_custom_call" | custom-call | tf_op jit(solution)/shard_map/shared/pallas_call | solution.py:678
  75.4 0.9 copy-done.6
  76.7 25.1 %group0.1 = (bf16[2,1024,512]{2,1,0:T(8,128)(2,1)}, bf16[2,1024,512]{2,1,0:T(8,128)(2,1)}, bf16[2,1024,512]{2,1,0:T(8,128)(2,1)}) custom-call(s32[16]{0:T(128)} %lengths.7, s32[4]{0:T(128)} %pad_add_fusion.info, s32[4]{0:T(128)} %get-tuple-element.60.flags, bf16[1056,1024]{1,0:T(8,128)(2,1)} %get-tuple-element.61.normed, ...), custom_call_target="tpu_custom_call" | custom-call | tf_op jit(solution)/shard_map/group0/pallas_call | solution.py:678
  101.9 0.8 copy-done.11
  102.7 1.6 collective-permute-start.13
  104.8 4.1 %carries.1 = bf16[4,2,128,512]{3,2,1,0:T(8,128)(2,1)} custom-call(s32[4]{0:T(128)} %pad_add_fusion.info, bf16[8,144,512]{2,1,0:T(8,128)(2,1)} %copy-done.1, f32[4,128,512]{2,1,0:T(8,128)} %get-tuple-element.77.ends, f32[4,128,512]{2,1,0:T(8,128)} %get-tuple-element.78.begins, f32[4,16,512]{2,1,0:T(8,128)} %get-tuple-element.79.passes), custom_call_target="tpu_custom_call" | custom-call | tf_op jit(solution)/shard_map/carries/pallas_call | solution.py:678
  109.0 3.8 %all-to-all-start.1 = ((bf16[4,2,128,512]{3,2,1,0:T(8,128)(2,1)}), bf16[4,2,128,512]{3,2,1,0:T(8,128)(2,1)S(1)}, u32[]{:S(2)}, u32[]{:S(2)}) async-start(bf16[4,2,128,512]{3,2,1,0:T(8,128)(2,1)} %carries.1), calls=%async_computation.1 | async-start | bytes 2097152 | tf_op jit(solution)/shard_map/all_to_all | solution.py:962
  113.3 6.6 %collective-permute-done.15.refs_24_ = bf16[256,1024]{1,0:T(8,128)(2,1)} collective-permute-done((bf16[256,1024]{1,0:T(8,128)(2,1)}, bf16[256,1024]{1,0:T(8,128)(2,1)}, u32[]{:S(2)}, u32[]{:S(2)}) %collective-permute-start.15) | collective-permute-done | bytes 524320 | tf_op jit(solution)/shard_map/ppermute | solution.py:696
  120.7 25.0 %group2.1 = (bf16[2,1024,512]{2,1,0:T(8,128)(2,1)}, bf16[2,1024,512]{2,1,0:T(8,128)(2,1)}, bf16[2,1024,512]{2,1,0:T(8,128)(2,1)}) custom-call(s32[16]{0:T(128)} %lengths.7, s32[4]{0:T(128)} %pad_add_fusion.info, s32[4]{0:T(128)} %get-tuple-element.60.flags, bf16[1056,1024]{1,0:T(8,128)(2,1)} %get-tuple-element.61.normed, ...), custom_call_target="tpu_custom_call" | custom-call | tf_op jit(solution)/shard_map/group2/pallas_call | solution.py:678
  145.8 0.9 copy-done.5
  147.1 16.9 %finish.1 = bf16[1024,1024]{1,0:T(8,128)(2,1)} custom-call(s32[4]{0:T(128)} %pad_add_fusion.info, bf16[4096,1024]{1,0:T(8,128)(2,1)} %refs_0_.1, bf16[1024,256]{1,0:T(8,128)(2,1)} %get-tuple-element.52.refs_1_, bf16[1024,128]{1,0:T(8,128)(2,1)} %get-tuple-element.53.refs_2_, bf16[1024,128]{1,0:T(8,128)(2,1)} %get-tuple-element.54.refs_3_, ...), custom_call_target="tpu_custom_call" | custom-call | tf_op jit(solution)/shard_map/finish/pallas_call | solution.py:678
  (84 shorter events, 7.0 us)
Async XLA Ops:
  0.0 10.8 %copy-start.20 = (bf16[1024]{0:T(1024)(128)(2,1)S(1)}, bf16[1024]{0:T(1024)(128)(2,1)}, u32[]{:S(2)}) copy-start(bf16[1024]{0:T(1024)(128)(2,1)} %param.15) | copy-start | bytes 6148
  1.4 22.3 %collective-permute-start.3 = (bf16[512,512]{1,0:T(8,128)(2,1)S(1)}, bf16[512,512]{1,0:T(8,128)(2,1)}, u32[]{:S(2)}, u32[]{:S(2)}) collective-permute-start(bf16[512,512]{1,0:T(8,128)(2,1)S(1)} %get-tuple-element.96), channel_id=1, source_target_pairs={{0,2},{1,3},{2,0},{3,1},{4,6},{5,7},{6,4},{7,5},{8,10},{9,11},{10,... | collective-permute-start | bytes 1572872 | tf_op jit(solution)/shard_map/ppermute | solution.py:696
  4.7 56.0 %copy-start.4 = (f32[16,1024]{1,0:T(8,128)}, f32[16,1024]{1,0:T(8,128)S(1)}, u32[]{:S(2)}) copy-start(f32[16,1024]{1,0:T(8,128)S(1)} %concatenate.3.refs_0_.refs_5_) | copy-start | bytes 196612
  4.7 18.9 %collective-permute-start.2 = (f32[16,1024]{1,0:T(8,128)S(1)}, f32[16,1024]{1,0:T(8,128)S(1)}, u32[]{:S(2)}, u32[]{:S(2)}) collective-permute-start(f32[16,1024]{1,0:T(8,128)S(1)} %concatenate.3.refs_0_.refs_5_), channel_id=1, source_target_pairs={{0,2},{1,3},{2,0},{3,1},{4,6},{5,7},{6,4},{7,5},{8,10},{9,11},{10,... | collective-permute-start | bytes 196616 | tf_op jit(solution)/shard_map/ppermute | solution.py:696
  5.6 18.0 %collective-permute-start = (bf16[16,1024]{1,0:T(8,128)(2,1)S(1)}, bf16[16,1024]{1,0:T(8,128)(2,1)S(1)}, u32[]{:S(2)}, u32[]{:S(2)}) collective-permute-start(bf16[16,1024]{1,0:T(8,128)(2,1)S(1)} %get-tuple-element.92), channel_id=1, source_target_pairs={{0,4},{4,8},{8,12},{12,16},{16,20},{20,24},{24,28},{1,5},{5,9},{9,... | collective-permute-start | bytes 98312 | tf_op jit(solution)/shard_map/ppermute | solution.py:747
  9.5 14.1 %collective-permute-start.1 = (bf16[16,1024]{1,0:T(8,128)(2,1)S(1)}, bf16[16,1024]{1,0:T(8,128)(2,1)S(1)}, u32[]{:S(2)}, u32[]{:S(2)}) collective-permute-start(bf16[16,1024]{1,0:T(8,128)(2,1)S(1)} %get-tuple-element.91), channel_id=1, source_target_pairs={{4,0},{8,4},{12,8},{16,12},{20,16},{24,20},{28,24},{5,1},{9,5},{13... | collective-permute-start | bytes 98312 | tf_op jit(solution)/shard_map/ppermute | solution.py:748
  23.6 38.4 %copy-start.8 = (f32[16,1024]{1,0:T(8,128)}, f32[16,1024]{1,0:T(8,128)S(1)}, u32[]{:S(2)}) copy-start(f32[16,1024]{1,0:T(8,128)S(1)} %collective-permute-done.2.refs_2_.refs_0_.refs_7_) | copy-start | bytes 196612
  23.7 24.8 %collective-permute-start.6 = (bf16[512,512]{1,0:T(8,128)(2,1)S(1)}, bf16[512,512]{1,0:T(8,128)(2,1)S(1)}, u32[]{:S(2)}, u32[]{:S(2)}) collective-permute-start(bf16[512,512]{1,0:T(8,128)(2,1)S(1)} %get-tuple-element.55), channel_id=1, source_target_pairs={{0,2},{1,3},{2,0},{3,1},{4,6},{5,7},{6,4},{7,5},{8,10},{9,11},{10,... | collective-permute-start | bytes 1572872 | tf_op jit(solution)/shard_map/ppermute | solution.py:696
  48.5 9.9 %copy-start.2 = (bf16[512,1024]{1,0:T(8,128)(2,1)S(1)}, bf16[512,1024]{1,0:T(8,128)(2,1)}, u32[]{:S(2)}) copy-start(bf16[512,1024]{1,0:T(8,128)(2,1)} %refs_21_) | copy-start | bytes 3145732
  49.3 53.4 %all-to-all-start = ((bf16[8,144,512]{2,1,0:T(8,128)(2,1)}), bf16[8,144,512]{2,1,0:T(8,128)(2,1)S(1)}, u32[]{:S(2)}, u32[]{:S(2)}) async-start(bf16[8,144,512]{2,1,0:T(8,128)(2,1)} %get-tuple-element.59), calls=%async_computation | async-start | bytes 2359296 | tf_op jit(solution)/shard_map/all_to_all | solution.py:857
  57.3 18.0 %collective-permute-start.7 = (bf16[1024,512]{1,0:T(8,128)(2,1)S(1)}, bf16[1024,512]{1,0:T(8,128)(2,1)S(1)}, u32[]{:S(2)}, u32[]{:S(2)}) collective-permute-start(bf16[1024,512]{1,0:T(8,128)(2,1)S(1)} %copy-done), channel_id=1, source_target_pairs={{0,1},{1,0},{2,3},{3,2},{4,5},{5,4},{6,7},{7,6},{8,9},{9,8},{10,11... | collective-permute-start | bytes 3145736 | tf_op jit(solution)/shard_map/ppermute | solution.py:696
  57.4 18.0 %collective-permute-start.8 = (bf16[1024,512]{1,0:T(8,128)(2,1)}, bf16[1024,512]{1,0:T(8,128)(2,1)S(1)}, u32[]{:S(2)}, u32[]{:S(2)}) collective-permute-start(bf16[1024,512]{1,0:T(8,128)(2,1)} %refs_3_), channel_id=1, source_target_pairs={{0,1},{1,0},{2,3},{3,2},{4,5},{5,4},{6,7},{7,6},{8,9},{9,8},{10,11... | collective-permute-start | bytes 3145736 | tf_op jit(solution)/shard_map/ppermute | solution.py:696
  57.9 44.8 %collective-permute-start.10 = (bf16[1024,512]{1,0:T(8,128)(2,1)}, bf16[1024,512]{1,0:T(8,128)(2,1)}, u32[]{:S(2)}, u32[]{:S(2)}) collective-permute-start(bf16[1024,512]{1,0:T(8,128)(2,1)} %refs_3_), channel_id=1, source_target_pairs={{0,2},{1,3},{2,0},{3,1},{4,6},{5,7},{6,4},{7,5},{8,10},{9,11},{10,... | collective-permute-start | bytes 3145736 | tf_op jit(solution)/shard_map/ppermute | solution.py:696
  59.3 42.6 %collective-permute-start.9 = (bf16[256,1024]{1,0:T(8,128)(2,1)S(1)}, bf16[256,1024]{1,0:T(8,128)(2,1)S(1)}, u32[]{:S(2)}, u32[]{:S(2)}) collective-permute-start(bf16[256,1024]{1,0:T(8,128)(2,1)S(1)} %get-tuple-element.94), channel_id=1, source_target_pairs={{0,2},{1,3},{2,0},{3,1},{4,6},{5,7},{6,4},{7,5},{8,10},{9,11},{10,... | collective-permute-start | bytes 1572872 | tf_op jit(solution)/shard_map/ppermute | solution.py:696
  60.8 1.3 collective-permute-start.4
  62.0 1.3 collective-permute-start.5
  102.7 17.2 %collective-permute-start.13 = (bf16[1024,512]{1,0:T(8,128)(2,1)}, bf16[1024,512]{1,0:T(8,128)(2,1)}, u32[]{:S(2)}, u32[]{:S(2)}) collective-permute-start(bf16[1024,512]{1,0:T(8,128)(2,1)} %collective-permute-done.10.refs_4_), channel_id=1, source_target_pairs={{0,1},{1,0},{2,3},{3,2},{4,5},{5,4},{6,7},{7,6},{8,9},{9,8},{10,11... | collective-permute-start | bytes 3145736 | tf_op jit(solution)/shard_map/ppermute | solution.py:696
  104.3 8.9 %collective-permute-start.11 = (bf16[512,512]{1,0:T(8,128)(2,1)}, bf16[512,512]{1,0:T(8,128)(2,1)}, u32[]{:S(2)}, u32[]{:S(2)}) collective-permute-start(bf16[512,512]{1,0:T(8,128)(2,1)} %collective-permute-done.3.refs_2_), channel_id=1, source_target_pairs={{0,1},{1,0},{2,3},{3,2},{4,5},{5,4},{6,7},{7,6},{8,9},{9,8},{10,11... | collective-permute-start | bytes 1572872 | tf_op jit(solution)/shard_map/ppermute | solution.py:696
  104.4 41.4 %collective-permute-start.14 = (bf16[512,1024]{1,0:T(8,128)(2,1)S(1)}, bf16[512,1024]{1,0:T(8,128)(2,1)S(1)}, u32[]{:S(2)}, u32[]{:S(2)}) collective-permute-start(bf16[512,1024]{1,0:T(8,128)(2,1)S(1)} %copy-done.2), channel_id=1, source_target_pairs={{0,1},{1,0},{2,3},{3,2},{4,5},{5,4},{6,7},{7,6},{8,9},{9,8},{10,11... | collective-permute-start | bytes 3145736 | tf_op jit(solution)/shard_map/ppermute | solution.py:696
  104.8 15.1 %collective-permute-start.15 = (bf16[256,1024]{1,0:T(8,128)(2,1)}, bf16[256,1024]{1,0:T(8,128)(2,1)}, u32[]{:S(2)}, u32[]{:S(2)}) collective-permute-start(bf16[256,1024]{1,0:T(8,128)(2,1)} %get-tuple-element.90), channel_id=1, source_target_pairs={{0,2},{1,3},{2,0},{3,1},{4,6},{5,7},{6,4},{7,5},{8,10},{9,11},{10,... | collective-permute-start | bytes 1572872 | tf_op jit(solution)/shard_map/ppermute | solution.py:696
  109.0 36.8 %all-to-all-start.1 = ((bf16[4,2,128,512]{3,2,1,0:T(8,128)(2,1)}), bf16[4,2,128,512]{3,2,1,0:T(8,128)(2,1)S(1)}, u32[]{:S(2)}, u32[]{:S(2)}) async-start(bf16[4,2,128,512]{3,2,1,0:T(8,128)(2,1)} %carries.1), calls=%async_computation.1 | async-start | bytes 2097152 | tf_op jit(solution)/shard_map/all_to_all | solution.py:962
  112.8 7.2 %collective-permute-start.12 = (bf16[512,512]{1,0:T(8,128)(2,1)}, bf16[512,512]{1,0:T(8,128)(2,1)S(1)}, u32[]{:S(2)}, u32[]{:S(2)}) collective-permute-start(bf16[512,512]{1,0:T(8,128)(2,1)} %copy-done.12), channel_id=1, source_target_pairs={{0,1},{1,0},{2,3},{3,2},{4,5},{5,4},{6,7},{7,6},{8,9},{9,8},{10,11... | collective-permute-start | bytes 1572872 | tf_op jit(solution)/shard_map/ppermute | solution.py:696
  113.2 32.5 %collective-permute-start.16 = (bf16[256,1024]{1,0:T(8,128)(2,1)}, bf16[256,1024]{1,0:T(8,128)(2,1)}, u32[]{:S(2)}, u32[]{:S(2)}) collective-permute-start(bf16[256,1024]{1,0:T(8,128)(2,1)} %copy-done.11), channel_id=1, source_target_pairs={{0,1},{1,0},{2,3},{3,2},{4,5},{5,4},{6,7},{7,6},{8,9},{9,8},{10,11... | collective-permute-start | bytes 1572872 | tf_op jit(solution)/shard_map/ppermute | solution.py:696
  119.9 25.9 %collective-permute-start.17 = (bf16[256,1024]{1,0:T(8,128)(2,1)}, bf16[256,1024]{1,0:T(8,128)(2,1)}, u32[]{:S(2)}, u32[]{:S(2)}) collective-permute-start(bf16[256,1024]{1,0:T(8,128)(2,1)} %collective-permute-done.15.refs_24_), channel_id=1, source_target_pairs={{0,1},{1,0},{2,3},{3,2},{4,5},{5,4},{6,7},{7,6},{8,9},{9,8},{10,11... | collective-permute-start | bytes 1572872 | tf_op jit(solution)/shard_map/ppermute | solution.py:696
  (19 other events, 51.7 us)

commit v2 on v1

--- a/solution.py
+++ b/solution.py
@@ -140,7 +140,10 @@
 
 def convolve_block(win, offset, taps, starts, first, put):
     convolve(win, offset, taps, None, put)
-
+    convolve_cut(win, offset, taps, starts, first, put)
+
+
+def convolve_cut(win, offset, taps, starts, first, put):
     @pl.when(has_cut(starts, first - (CONV - 2), first + BLOCK + CONV - 2))
     def _():
         shape = (SUB, LANES)
@@ -170,6 +173,21 @@
     out = dot(normed, joined[...])
     mix[...] = out[:, : inner + STATE].astype(bf16)
     steps[...] = softplus(out[:, inner + STATE :] + row[...])
+
+
+def pack_kernel(heads, inner, step_w, conv, gain, skip, bias, decay_log, out):
+    out[...] = jnp.zeros_like(out)
+    out[:heads, :] = step_w[...].astype(f32)
+    out[heads : heads + CONV, :inner] = conv[...].astype(f32)
+    row = heads + CONV
+    out[row : row + 1, :inner] = gain[...].astype(f32)
+    wide = jnp.zeros((1, inner), f32)
+    head = lax.div(iota((1, inner), 1), HEAD_DIM)
+    for h in range(heads):
+        wide = jnp.where(head == h, jnp.broadcast_to(skip[:, h : h + 1], (1, inner)), wide)
+    out[row + 1 : row + 2, :inner] = wide
+    out[row + 2 : row + 3, :heads] = bias[...]
+    out[row + 3 : row + 4, :heads] = decay_log[...]
 
 
 def state_kernel(
@@ -242,9 +260,10 @@
 
     end_state = jnp.zeros((STATE, inner), f32)
     begin_state = jnp.zeros((STATE, inner), f32)
-    for c in range(blocks):
-        at = pl.ds(c * BLOCK, BLOCK)
-        tile_up(win, pl.ds(HALO, BLOCK), mix[at, :].astype(f32))
+    def prepare(c):
+        slot = c & 1
+        here_win = win.at[slot]
+        tile_up(here_win, pl.ds(HALO, BLOCK), mix[pl.ds(c * BLOCK, BLOCK), :].astype(f32))
         if c == 0:
             ahead = jnp.where(quarter == 0, edge[:HALO], before[...].astype(f32))
         else:
@@ -253,27 +272,34 @@
             behind = jnp.where(quarter == quarters - 1, edge[HALO:], after[...].astype(f32))
         else:
             behind = mix[(c + 1) * BLOCK : (c + 1) * BLOCK + HALO, :].astype(f32)
-
-        tile_up(win, pl.ds(0, HALO), ahead)
-        tile_up(win, pl.ds(HALO + BLOCK, HALO), behind)
+        tile_up(here_win, pl.ds(0, HALO), ahead)
+        tile_up(here_win, pl.ds(HALO + BLOCK, HALO), behind)
 
         def put(tile, at, forward, backward):
-            xf[tile, at, :] = forward
-            xb[tile, at, :] = backward
-
-        here = first + c * BLOCK
-        convolve_block(win, 0, taps, starts, here, put)
+            xf[slot, tile, at, :] = forward
+            xb[slot, tile, at, :] = backward
+
+        convolve(here_win, 0, taps, None, put)
+        return functools.partial(convolve_cut, here_win, 0, taps, starts, first + c * BLOCK, put)
+
+    prepare(0)()
+    for c in range(blocks):
+        repair = prepare(c + 1) if c + 1 < blocks else None
+        at = pl.ds(c * BLOCK, BLOCK)
+        here_f, here_b = xf.at[c & 1], xb.at[c & 1]
         dt = steps[at, :]
         inclusive = sums[at, :]
         weight_f = dt * jnp.exp(total - inclusive)
         weight_b = dt * jnp.exp(inclusive + dt * rate[...])
-        position = iota((BLOCK, 1), 0) + here
+        position = iota((BLOCK, 1), 0) + first + c * BLOCK
         spread_f = dot(halves_of(weight_f), pick[...])
         spread_b = dot(halves_of(weight_b), pick[...])
-        write_f = jnp.where(position >= last_start, xf[value_tiles, :BLOCK], 0.0).astype(bf16)
-        write_b = jnp.where(position < first_end, xb[value_tiles, :BLOCK], 0.0).astype(bf16)
-        end_state += dot_first(write_f, (side_by_side(xf.at[:value_tiles]) * spread_f).astype(bf16))
-        begin_state += dot_first(write_b, (side_by_side(xb.at[:value_tiles]) * spread_b).astype(bf16))
+        write_f = jnp.where(position >= last_start, here_f[value_tiles, :BLOCK], 0.0).astype(bf16)
+        write_b = jnp.where(position < first_end, here_b[value_tiles, :BLOCK], 0.0).astype(bf16)
+        end_state += dot_first(write_f, (side_by_side(here_f.at[:value_tiles]) * spread_f).astype(bf16))
+        begin_state += dot_first(write_b, (side_by_side(here_b.at[:value_tiles]) * spread_b).astype(bf16))
+        if repair is not None:
+            repair()
 
     ends[0] = end_state
     begins[0] = begin_state
@@ -471,48 +497,55 @@
             enter[at, :] = jnp.where(entered, reads, 0.0).astype(bf16)
 
 
-def group_kernel(
-    group,
-    split,
-    group_heads,
-    heads,
-    pieces,
-    lengths,
-    info,
-    flags,
-    normed,
-    factors,
-    raw,
-    raw_t,
-    mix_f,
-    mix_b,
-    write_f,
-    write_b,
-    read_f,
-    read_b,
-    *refs,
-):
+def group_kernel(group, split, group_heads, heads, pieces, lengths, info, flags, *refs):
     members = len(split)
     count = sum(sum(pair) for pair in split)
-    smalls, weights, refs = refs[:members], refs[members : members + count], refs[members + count :]
-    out_f, out_b, gate_out, held, sems, win, xf, xb, acc, state_f, state_b, pick, taps, skip = refs
+    smalls, refs = refs[:members], refs[members:]
+    raw_far, raw_t_far = refs[:2]
+    shared_far, refs = refs[2:10], refs[10:]
+    weights, refs = refs[:count], refs[count:]
+    out_f, out_b, gate_out, held, sems = refs[:5]
+    normed, factors, mix_f, mix_b, write_f, write_b, read_f, read_b = refs[5:13]
+    raw, raw_t, win, xf, xb, acc, state_f, state_b, pick, taps, skip = refs[13:]
     step = pl.program_id(0)
-    copies, owners, at = [], [], 0
+    copies, at = {}, 0
     for k, pair in enumerate(split):
         for which, number in enumerate(pair):
             row = 0
+            copies[k, which] = []
             for _ in range(number):
                 size = weights[at].shape[0]
                 target = held.at[2 * k + which, row : row + size]
-                copies.append(pltpu.make_async_copy(weights[at], target, sems.at[at]))
-                owners.append(k)
+                copies[k, which].append(pltpu.make_async_copy(weights[at], target, sems.at[at]))
                 row += size
                 at += 1
+    near = refs[5:13]
+    shared = [
+        pltpu.make_async_copy(far, here, sems.at[count + k])
+        for k, (far, here) in enumerate(zip(shared_far, near))
+    ]
+
+    def start(some):
+        for copy in some:
+            copy.start()
+
+    def wait(some):
+        for copy in some:
+            copy.wait()
 
     @pl.when(step == 0)
     def _():
-        for copy in copies:
-            copy.start()
+        start(shared[:1] + copies[0, 0])
+        wait(shared[:1] + copies[0, 0])
+        start(copies[0, 1] + shared[1:])
+        for k in range(1, members):
+            start(copies[k, 0] + copies[k, 1])
+
+    for k in range(1, members):
+
+        @pl.when(step == k)
+        def _():
+            wait(copies[k, 0] + copies[k, 1])
 
     out_f, out_b, gate_out = (r.at[0] for r in (out_f, out_b, gate_out))
     value_w, gate_w = held.at[2 * step], held.at[2 * step + 1]
@@ -530,11 +563,12 @@
         def _():
             taps[...] = smalls[k][group_heads : group_heads + CONV, :inner] * 0.5
             skip[...] = smalls[k][group_heads + CONV + 1 : group_heads + CONV + 2, :inner]
-            for copy, owner in zip(copies, owners):
-                if owner == k:
-                    copy.wait()
 
     tile_up(win, slice(None), dot(normed[...], value_w[...]).astype(bf16).astype(f32))
+
+    @pl.when(step == 0)
+    def _():
+        wait(copies[0, 1] + shared[1:])
 
     def prepare(c, unused):
         at = pl.ds(pl.multiple_of(c * BLOCK, BLOCK), BLOCK)
@@ -577,10 +611,12 @@
         at = pl.ds(pl.multiple_of(c * BLOCK, BLOCK), BLOCK)
         grow = dot(factors[at, :], pick[kind])
         carried = state[now]
+        pltpu.sync_copy(raw_far.at[at, :], raw)
+        pltpu.sync_copy(raw_t_far.at[c], raw_t)
         pairs = mix[c].astype(f32)
         lane = iota((1, LANES), 1)
         half = lane >= HEAD_DIM
-        values = raw[at, :]
+        values = raw[...]
 
         def pair(p, unused):
             cols = pl.ds(pl.multiple_of(p * LANES, LANES), LANES)
@@ -589,8 +625,8 @@
             for side in range(LANES // HEAD_DIM):
                 head = offset + p * (LANES // HEAD_DIM) + side
                 down = jnp.sum(jnp.where(lane == head + kind * heads, values, 0.0), axis=1, keepdims=True)
-                across = raw_t[c, pl.ds(head + kind * heads, 1), :]
-                head_steps = raw_t[c, pl.ds(head + heads, 1), :]
+                across = raw_t[pl.ds(head + kind * heads, 1), :]
+                head_steps = raw_t[pl.ds(head + heads, 1), :]
                 table = pairs * jnp.exp(jnp.minimum(down - across, 0.0)) * head_steps
                 sums.append(dot(table.astype(bf16), x_pair))
             acc[:, cols] = jnp.where(half, sums[1], sums[0])
@@ -709,11 +745,6 @@
     return held
 
 
-def cut_rows(x):
-    middle = x.shape[0] // 2
-    return x[:middle], x[middle:]
-
-
 def local(
     hidden_in,
     norm_gain,
@@ -747,14 +778,21 @@
     before = lax.ppermute(hidden_in[-HALO:], "seq", up)
     after = lax.ppermute(hidden_in[:HALO], "seq", down)
     small = [step_weight.T, conv_value, output_gain.reshape(1, -1)]
-    small += [jnp.repeat(skip_gain, HEAD_DIM).reshape(1, -1), step_bias.reshape(1, -1)]
-    small += [decay_log.reshape(1, -1)]
-    small = jnp.concatenate(
-        [jnp.pad(a.astype(f32), ((0, 0), (0, width - a.shape[1]))) for a in small], axis=0
+    small += [a.reshape(1, -1) for a in (skip_gain, step_bias, decay_log)]
+    small_rows = -(-(group_heads + CONV + 4) // SUB) * SUB
+    small = call(
+        functools.partial(pack_kernel, group_heads, inner),
+        (1,),
+        (),
+        small,
+        [whole(a.shape) for a in small],
+        struct((small_rows, width), f32),
+        whole((small_rows, width)),
+        [],
+        "small",
     )
     far_smalls = from_far(small, groups)
-    value_first, value_second = cut_rows(value_weight)
-    far_first = from_far(value_first, groups)
+    far_values = from_far(value_weight, groups)
     info = jnp.stack([place * tokens, place, place * tokens + me * rows, me]).astype(jnp.int32)
     gain = norm_gain.reshape(1, width)
 
@@ -778,10 +816,10 @@
         [pltpu.VMEM((width, columns + LANES), bf16), pltpu.VMEM((1, LANES), f32)],
         "project",
     )
-    before, after, far_smalls, far_first, value_second, mix = lax.optimization_barrier(
-        (before, after, far_smalls, far_first, value_second, mix)
+    before, after, far_smalls, far_values, gate_weight, mix = lax.optimization_barrier(
+        (before, after, far_smalls, far_values, gate_weight, mix)
     )
-    far_second = from_far(value_second, groups)
+    far_gates = from_far(gate_weight, groups)
     per = rows // HALO
     state_shape = (groups, STATE, inner)
     one_state = pl.BlockSpec((1, STATE, inner), lambda i, *_: (i, 0, 0))
@@ -833,9 +871,9 @@
         ],
         [
             pltpu.VMEM((2 * HALO, columns), f32),
-            pltpu.VMEM((columns // LANES, WINDOW, LANES), f32),
-            pltpu.VMEM((columns // LANES, COVER, LANES), f32),
-            pltpu.VMEM((columns // LANES, COVER, LANES), f32),
+            pltpu.VMEM((2, columns // LANES, WINDOW, LANES), f32),
+            pltpu.VMEM((2, columns // LANES, COVER, LANES), f32),
+            pltpu.VMEM((2, columns // LANES, COVER, LANES), f32),
             pltpu.VMEM((rows, LANES), f32),
             pltpu.VMEM((STATE + SUB, inner), f32),
             pltpu.VMEM((STATE + SUB, inner), f32),
@@ -846,14 +884,12 @@
         "states",
     )
 
-    far_second, sent, gate_weight, output_weight = lax.optimization_barrier(
-        (far_second, sent, gate_weight, output_weight)
+    values = gather_near(value_weight, [far_values], groups)
+    smalls = [piece[0] for piece in gather_near(small, [far_smalls], groups)]
+    far_gates, sent, output_weight, values, smalls = lax.optimization_barrier(
+        (far_gates, sent, output_weight, values, smalls)
     )
-    values = gather_near(value_weight, [far_first, far_second], groups)
-    smalls = [piece[0] for piece in gather_near(small, [far_smalls], groups)]
-    far_gates = from_far(gate_weight, groups)
-    out_first, out_second = cut_rows(output_weight)
-    far_out_first = from_far(out_first, groups)
+    far_outs = from_far(output_weight, groups)
     got = lax.all_to_all(sent, "seq", split_axis=0, concat_axis=0, tiled=True)
 
     near_shape = (rows + 2 * HALO, width)
@@ -910,8 +946,8 @@
     done = []
 
     def do_groups(g):
-        arrays = (normed, factors, raw, raw_t, mix_f, mix_b, write_f, write_b, read_f, read_b)
-        arrays += tuple(smalls[g : g + members])
+        small = tuple(smalls[g : g + members])
+        arrays = (normed, factors, mix_f, mix_b, write_f, write_b, read_f, read_b)
         loaded = [values[k] + gates[k] for k in range(g, g + members)]
         split = [(len(values[k]), len(gates[k])) for k in range(g, g + members)]
         loaded = [w for ws in loaded for w in ws]
@@ -920,13 +956,19 @@
                 functools.partial(group_kernel, g, split, group_heads, heads, pieces),
                 (members,),
                 (piece_lengths, info, flags),
-                arrays + tuple(loaded),
-                [whole(a.shape) for a in arrays] + [pl.BlockSpec(memory_space=pl.ANY)] * len(loaded),
+                small + (raw, raw_t) + arrays + tuple(loaded),
+                [whole(a.shape) for a in small]
+                + [pl.BlockSpec(memory_space=pl.ANY)] * (2 + len(arrays) + len(loaded)),
                 [struct((members, rows, inner), bf16)] * 3,
                 [pl.BlockSpec((1, rows, inner), lambda i, *_: (i, 0, 0))] * 3,
                 [
                     pltpu.VMEM((2 * members, width, inner), bf16),
-                    pltpu.SemaphoreType.DMA((len(loaded),)),
+                    pltpu.SemaphoreType.DMA((len(loaded) + len(arrays),)),
+                ]
+                + [pltpu.VMEM(a.shape, a.dtype) for a in arrays]
+                + [
+                    pltpu.VMEM((BLOCK, LANES), f32),
+                    pltpu.VMEM((LANES, BLOCK), f32),
                     pltpu.VMEM((inner // LANES, rows + 2 * HALO, LANES), f32),
                     pltpu.VMEM((blocks, inner // LANES, COVER, LANES), f32),
                     pltpu.VMEM((blocks, inner // LANES, COVER, LANES), f32),
@@ -943,11 +985,8 @@
 
     gates = [[gate_weight], [swap(gate_weight, "head", 1)]][:groups]
     do_groups(0)
-    got, done[0], far_out_first, far_gates, out_second = lax.optimization_barrier(
-        (got, done[0], far_out_first, far_gates, out_second)
-    )
+    got, done[0], far_outs = lax.optimization_barrier((got, done[0], far_outs))
     gates += gather_near(gate_weight, [far_gates], groups)[members:]
-    far_out_second = from_far(out_second, groups)
     entering = call(
         functools.partial(carry_kernel, places, groups),
         (1,),
@@ -963,7 +1002,7 @@
 
     for g in range(members, groups, members):
         do_groups(g)
-    outs = gather_near(output_weight, [far_out_first, far_out_second], groups)
+    outs = gather_near(output_weight, [far_outs], groups)
 
     tile = min(512, rows)
     tiles = rows // tile

time: 166 us -> 151 us (0.910)
  waiting for transfers between devices: 8.98 us -> 2.8 us
  starting transfers between devices: 27.1 us -> 22.3 us
  local copies, waits for them, and re-layouts: 9.47 us -> 6.25 us
    ppermute x16 -> x12, waiting for transfers between devices: 8.97 us -> 2.79 us  [swap(): lax.ppermute(x, axis, [(i, i ^ distance) for i in range(lax.axis_size(axi...]
    ppermute x16 -> x12, starting transfers between devices: 10.2 us -> 7.02 us  [swap(): lax.ppermute(x, axis, [(i, i ^ distance) for i in range(lax.axis_size(axi...]
    unnamed x46 -> x26, local copies, waits for them, and re-layouts: 5.69 us -> 2.94 us
    slice x2 -> x0, local copies, waits for them, and re-layouts: 2.19 us -> none  [cut_rows(): return (x[:middle], x[middle:])]
    all_to_all x1, starting transfers between devices: 8.03 us -> 6.35 us  [local(): got = lax.all_to_all(sent, 'seq', split_axis=0, concat_axis=0, tiled=True)]
    pallas_call x7 -> x8, Pallas kernels: 117 us -> 118 us  [call(): pl.pallas_call(kernel, grid_spec=pltpu.PrefetchScalarGridSpec(num_scalar_...]
  transfers between devices with their start and end apart: 20 -> 16, of which waited for: 3 -> 2; matrix products, arithmetic and copies ran while one was open for 2% -> 3% of each run, Pallas kernels for 61% -> 67%
where the time goes in v2:
time: 151 us; the launch traced here: 150 us
  Pallas kernels  118 us (78%)
  starting transfers between devices  22.3 us (15%)
  local copies, waits for them, and re-layouts  6.25 us (4%)
  waiting for transfers between devices  2.8 us (2%)
    pallas_call x8, Pallas kernels, call(): pl.pallas_call(kernel, grid_spec=pltpu.PrefetchScalarGridSpec(num_scalar_...  118 us
    ppermute x12, starting transfers between devices, swap(): lax.ppermute(x, axis, [(i, i ^ distance) for i in range(lax.axis_size(axi...  7.02 us
    all_to_all x1, starting transfers between devices, local(): got = lax.all_to_all(sent, 'seq', split_axis=0, concat_axis=0, tiled=True)  6.35 us
    ppermute x1, starting transfers between devices, local(): before = lax.ppermute(hidden_in[-HALO:], 'seq', up)  3.89 us
    all_to_all x1, starting transfers between devices, local(): lax.all_to_all(entering, 'head', split_axis=0, concat_axis=0, tiled=True)  3.74 us
  transfers between devices with their start and end apart: 16, of which 2 were waited for; matrix products, arithmetic and copies ran while one was open for 3% of the time, Pallas kernels for 67%

profile of v2, /device:TPU:0, one launch (start us, length us, event | category | flops | bytes accessed | tf_op | source)
XLA Modules:
  0.0 150.5 jit_solution(10296810953205196540)
XLA Ops:
  0.0 3.0 %collective-permute-start.3 = (bf16[1024,512]{1,0:T(8,128)(2,1)}, bf16[1024,512]{1,0:T(8,128)(2,1)S(1)}, u32[]{:S(2)}, u32[]{:S(2)}) collective-permute-start(bf16[1024,512]{1,0:T(8,128)(2,1)} %refs_12_), channel_id=1, source_target_pairs={{0,2},{1,3},{2,0},{3,1},{4,6},{5,7},{6,4},{7,5},{8,10},{9,11},{10,... | collective-permute-start | bytes 3145736 | tf_op jit(solution)/shard_map/ppermute | solution.py:732
  3.0 1.3 reshape.17.gain
  4.2 1.5 small.1.refs_0_.refs_5_
  5.7 0.8 fusion
  6.5 3.9 %collective-permute-start = (bf16[16,1024]{1,0:T(8,128)(2,1)S(1)}, bf16[16,1024]{1,0:T(8,128)(2,1)S(1)}, u32[]{:S(2)}, u32[]{:S(2)}) collective-permute-start(bf16[16,1024]{1,0:T(8,128)(2,1)S(1)} %get-tuple-element.102), channel_id=1, source_target_pairs={{0,4},{4,8},{8,12},{12,16},{16,20},{20,24},{24,28},{1,5},{5,9},{9,... | collective-permute-start | bytes 98312 | tf_op jit(solution)/shard_map/ppermute | solution.py:778
  10.4 1.3 collective-permute-start.1
  11.7 1.3 reshape.21.gain
  13.0 12.2 %project.1 = (bf16[4096,640]{1,0:T(8,128)(2,1)}, f32[4096,128]{1,0:T(8,128)}) custom-call(bf16[4096,1024]{1,0:T(8,128)(2,1)} %refs_0_.1, bf16[1,1024]{1,0:T(2,128)(2,1)} %reshape.21.gain, bf16[1024,512]{1,0:T(8,128)(2,1)} %refs_12_, bf16[1024,256]{1,0:T(8,128)(2,1)} %state_w.5, bf16[8,1024]{1,0:T(8,128)(2,1)} %bitcast.9, f32[1,8]{1,0:T(1,128)} %bitcast.11), custom_call_target="tpu_custom_call" | custom-call | tf_op jit(solution)/shard_map/project/pallas_call | solution.py:714
  25.3 2.4 %collective-permute-done.2.refs_2_.refs_0_.refs_7_ = f32[16,1024]{1,0:T(8,128)S(1)} collective-permute-done((f32[16,1024]{1,0:T(8,128)}, f32[16,1024]{1,0:T(8,128)S(1)}, u32[]{:S(2)}, u32[]{:S(2)}) %collective-permute-start.2) | collective-permute-done | bytes 65568 | tf_op jit(solution)/shard_map/ppermute | solution.py:732
  27.7 1.8 %collective-permute-start.4 = (bf16[1024,512]{1,0:T(8,128)(2,1)}, bf16[1024,512]{1,0:T(8,128)(2,1)S(1)}, u32[]{:S(2)}, u32[]{:S(2)}) collective-permute-start(bf16[1024,512]{1,0:T(8,128)(2,1)} %refs_13_), channel_id=1, source_target_pairs={{0,2},{1,3},{2,0},{3,1},{4,6},{5,7},{6,4},{7,5},{8,10},{9,11},{10,... | collective-permute-start | bytes 3145736 | tf_op jit(solution)/shard_map/ppermute | solution.py:732
  29.6 0.5 collective-permute-start.7
  30.1 0.6 pad_add_fusion.info
  30.7 21.2 %states.1 = (f32[4,128,512]{2,1,0:T(8,128)}, f32[4,128,512]{2,1,0:T(8,128)}, f32[4,16,512]{2,1,0:T(8,128)}, bf16[8,144,512]{2,1,0:T(8,128)(2,1)}) custom-call(s32[16]{0:T(128)} %lengths.7, s32[4]{0:T(128)} %pad_add_fusion.info, bf16[4096,640]{1,0:T(8,128)(2,1)} %get-tuple-element.57.mix.before.after, bf16[4096,640]{1,0:T(8,128)(2,1)} %get-tuple-element.57.mix.before.after, ...), custom_call_target="tpu_custom_call" | custom-call | tf_op jit(solution)/shard_map/states/pallas_call | solution.py:714
  52.4 6.4 %all-to-all-start = ((bf16[8,144,512]{2,1,0:T(8,128)(2,1)}), bf16[8,144,512]{2,1,0:T(8,128)(2,1)S(1)}, u32[]{:S(2)}, u32[]{:S(2)}) async-start(bf16[8,144,512]{2,1,0:T(8,128)(2,1)} %get-tuple-element.69), calls=%async_computation | async-start | bytes 2359296 | tf_op jit(solution)/shard_map/all_to_all | solution.py:893
  59.0 0.8 collective-permute-start.10
  60.3 11.6 %shared.1 = (bf16[1056,1024]{1,0:T(8,128)(2,1)}, bf16[1024,256]{1,0:T(8,128)(2,1)}, bf16[1024,256]{1,0:T(8,128)(2,1)}, f32[1024,128]{1,0:T(8,128)}, f32[4,128,25...) custom-call(s32[16]{0:T(128)} %lengths.7, ...), custom_call_target="tpu_custom_call" | custom-call | tf_op jit(solution)/shard_map/shared/pallas_call | solution.py:714
  71.9 1.0 copy-done.7
  72.9 25.3 %group0.1 = (bf16[2,1024,512]{2,1,0:T(8,128)(2,1)}, bf16[2,1024,512]{2,1,0:T(8,128)(2,1)}, bf16[2,1024,512]{2,1,0:T(8,128)(2,1)}) custom-call(s32[16]{0:T(128)} %lengths.7, s32[4]{0:T(128)} %pad_add_fusion.info, s32[4]{0:T(128)} %get-tuple-element.70.flags, f32[16,1024]{1,0:T(8,128)} %small.1.refs_0_.refs_5_, f32[16,1024]{1,0:T(8,128)} %copy-done.9, ...), custom_call_target="tpu_custom_call" | custom-call | tf_op jit(solution)/shard_map/group0/pallas_call | solution.py:714
  98.3 1.0 copy-done
  99.3 4.2 %carries.1 = bf16[4,2,128,512]{3,2,1,0:T(8,128)(2,1)} custom-call(s32[4]{0:T(128)} %pad_add_fusion.info, bf16[8,144,512]{2,1,0:T(8,128)(2,1)} %copy-done, f32[4,128,512]{2,1,0:T(8,128)} %get-tuple-element.88.ends, f32[4,128,512]{2,1,0:T(8,128)} %get-tuple-element.89.begins, f32[4,16,512]{2,1,0:T(8,128)} %get-tuple-element.90.passes), custom_call_target="tpu_custom_call" | custom-call | tf_op jit(solution)/shard_map/carries/pallas_call | solution.py:714
  103.4 3.7 %all-to-all-start.1 = ((bf16[4,2,128,512]{3,2,1,0:T(8,128)(2,1)}), bf16[4,2,128,512]{3,2,1,0:T(8,128)(2,1)S(1)}, u32[]{:S(2)}, u32[]{:S(2)}) async-start(bf16[4,2,128,512]{3,2,1,0:T(8,128)(2,1)} %carries.1), calls=%async_computation.1 | async-start | bytes 2097152 | tf_op jit(solution)/shard_map/all_to_all | solution.py:1001
  107.2 25.2 %group2.1 = (bf16[2,1024,512]{2,1,0:T(8,128)(2,1)}, bf16[2,1024,512]{2,1,0:T(8,128)(2,1)}, bf16[2,1024,512]{2,1,0:T(8,128)(2,1)}) custom-call(s32[16]{0:T(128)} %lengths.7, s32[4]{0:T(128)} %pad_add_fusion.info, s32[4]{0:T(128)} %get-tuple-element.70.flags, f32[16,1024]{1,0:T(8,128)} %copy-done.8, f32[16,1024]{1,0:T(8,128)} %copy-done.10, ...), custom_call_target="tpu_custom_call" | custom-call | tf_op jit(solution)/shard_map/group2/pallas_call | solution.py:714
  132.4 1.0 copy-done.1
  133.4 16.9 %finish.1 = bf16[1024,1024]{1,0:T(8,128)(2,1)} custom-call(s32[4]{0:T(128)} %pad_add_fusion.info, bf16[4096,1024]{1,0:T(8,128)(2,1)} %refs_0_.1, bf16[1024,256]{1,0:T(8,128)(2,1)} %get-tuple-element.66.refs_1_, bf16[1024,128]{1,0:T(8,128)(2,1)} %get-tuple-element.67.refs_2_, bf16[1024,128]{1,0:T(8,128)(2,1)} %get-tuple-element.68.refs_3_, ...), custom_call_target="tpu_custom_call" | custom-call | tf_op jit(solution)/shard_map/finish/pallas_call | solution.py:714
  (46 shorter events, 1.4 us)
Async XLA Ops:
  0.0 27.7 %collective-permute-start.3 = (bf16[1024,512]{1,0:T(8,128)(2,1)}, bf16[1024,512]{1,0:T(8,128)(2,1)S(1)}, u32[]{:S(2)}, u32[]{:S(2)}) collective-permute-start(bf16[1024,512]{1,0:T(8,128)(2,1)} %refs_12_), channel_id=1, source_target_pairs={{0,2},{1,3},{2,0},{3,1},{4,6},{5,7},{6,4},{7,5},{8,10},{9,11},{10,... | collective-permute-start | bytes 3145736 | tf_op jit(solution)/shard_map/ppermute | solution.py:732
  5.7 22.1 %collective-permute-start.2 = (f32[16,1024]{1,0:T(8,128)}, f32[16,1024]{1,0:T(8,128)S(1)}, u32[]{:S(2)}, u32[]{:S(2)}) collective-permute-start(f32[16,1024]{1,0:T(8,128)} %small.1.refs_0_.refs_5_), channel_id=1, source_target_pairs={{0,2},{1,3},{2,0},{3,1},{4,6},{5,7},{6,4},{7,5},{8,10},{9,11},{10,... | collective-permute-start | bytes 196616 | tf_op jit(solution)/shard_map/ppermute | solution.py:732
  6.5 18.8 %collective-permute-start = (bf16[16,1024]{1,0:T(8,128)(2,1)S(1)}, bf16[16,1024]{1,0:T(8,128)(2,1)S(1)}, u32[]{:S(2)}, u32[]{:S(2)}) collective-permute-start(bf16[16,1024]{1,0:T(8,128)(2,1)S(1)} %get-tuple-element.102), channel_id=1, source_target_pairs={{0,4},{4,8},{8,12},{12,16},{16,20},{20,24},{24,28},{1,5},{5,9},{9,... | collective-permute-start | bytes 98312 | tf_op jit(solution)/shard_map/ppermute | solution.py:778
  10.4 14.9 %collective-permute-start.1 = (bf16[16,1024]{1,0:T(8,128)(2,1)S(1)}, bf16[16,1024]{1,0:T(8,128)(2,1)S(1)}, u32[]{:S(2)}, u32[]{:S(2)}) collective-permute-start(bf16[16,1024]{1,0:T(8,128)(2,1)S(1)} %get-tuple-element.101), channel_id=1, source_target_pairs={{4,0},{8,4},{12,8},{16,12},{20,16},{24,20},{28,24},{5,1},{9,5},{13... | collective-permute-start | bytes 98312 | tf_op jit(solution)/shard_map/ppermute | solution.py:779
  11.7 40.4 %collective-permute-start.5 = (bf16[1024,512]{1,0:T(8,128)(2,1)}, bf16[1024,512]{1,0:T(8,128)(2,1)}, u32[]{:S(2)}, u32[]{:S(2)}) collective-permute-start(bf16[1024,512]{1,0:T(8,128)(2,1)} %refs_12_), channel_id=1, source_target_pairs={{0,1},{1,0},{2,3},{3,2},{4,5},{5,4},{6,7},{7,6},{8,9},{9,8},{10,11... | collective-permute-start | bytes 3145736 | tf_op jit(solution)/shard_map/ppermute | solution.py:732
  13.0 16.5 %copy-start.2 = (f32[16,1024]{1,0:T(8,128)S(1)}, f32[16,1024]{1,0:T(8,128)}, u32[]{:S(2)}) copy-start(f32[16,1024]{1,0:T(8,128)} %small.1.refs_0_.refs_5_) | copy-start | bytes 196612
  27.7 24.2 %copy-start.8 = (f32[16,1024]{1,0:T(8,128)}, f32[16,1024]{1,0:T(8,128)S(1)}, u32[]{:S(2)}) copy-start(f32[16,1024]{1,0:T(8,128)S(1)} %collective-permute-done.2.refs_2_.refs_0_.refs_7_) | copy-start | bytes 196612
  27.7 24.2 %copy-start.5 = (bf16[1024,512]{1,0:T(8,128)(2,1)}, bf16[1024,512]{1,0:T(8,128)(2,1)S(1)}, u32[]{:S(2)}) copy-start(bf16[1024,512]{1,0:T(8,128)(2,1)S(1)} %collective-permute-done.3.refs_12_) | copy-start | bytes 3145732
  27.7 24.6 %collective-permute-start.4 = (bf16[1024,512]{1,0:T(8,128)(2,1)}, bf16[1024,512]{1,0:T(8,128)(2,1)S(1)}, u32[]{:S(2)}, u32[]{:S(2)}) collective-permute-start(bf16[1024,512]{1,0:T(8,128)(2,1)} %refs_13_), channel_id=1, source_target_pairs={{0,2},{1,3},{2,0},{3,1},{4,6},{5,7},{6,4},{7,5},{8,10},{9,11},{10,... | collective-permute-start | bytes 3145736 | tf_op jit(solution)/shard_map/ppermute | solution.py:732
  29.6 22.8 %collective-permute-start.6 = (bf16[1024,512]{1,0:T(8,128)(2,1)S(1)}, bf16[1024,512]{1,0:T(8,128)(2,1)}, u32[]{:S(2)}, u32[]{:S(2)}) collective-permute-start(bf16[1024,512]{1,0:T(8,128)(2,1)S(1)} %collective-permute-done.3.refs_12_), channel_id=1, source_target_pairs={{0,1},{1,0},{2,3},{3,2},{4,5},{5,4},{6,7},{7,6},{8,9},{9,8},{10,11... | collective-permute-start | bytes 3145736 | tf_op jit(solution)/shard_map/ppermute | solution.py:732
  29.6 22.4 %collective-permute-start.7 = (f32[16,1024]{1,0:T(8,128)S(1)}, f32[16,1024]{1,0:T(8,128)S(1)}, u32[]{:S(2)}, u32[]{:S(2)}) collective-permute-start(f32[16,1024]{1,0:T(8,128)S(1)} %copy-done.2), channel_id=1, source_target_pairs={{0,1},{1,0},{2,3},{3,2},{4,5},{5,4},{6,7},{7,6},{8,9},{9,8},{10,11... | collective-permute-start | bytes 196616 | tf_op jit(solution)/shard_map/ppermute | solution.py:732
  30.1 22.0 %collective-permute-start.8 = (f32[16,1024]{1,0:T(8,128)S(1)}, f32[16,1024]{1,0:T(8,128)S(1)}, u32[]{:S(2)}, u32[]{:S(2)}) collective-permute-start(f32[16,1024]{1,0:T(8,128)S(1)} %collective-permute-done.2.refs_2_.refs_0_.refs_7_), channel_id=1, source_target_pairs={{0,1},{1,0},{2,3},{3,2},{4,5},{5,4},{6,7},{7,6},{8,9},{9,8},{10,11... | collective-permute-start | bytes 196616 | tf_op jit(solution)/shard_map/ppermute | solution.py:732
  52.0 7.0 %copy-start.3 = (bf16[512,1024]{1,0:T(8,128)(2,1)S(1)}, bf16[512,1024]{1,0:T(8,128)(2,1)}, u32[]{:S(2)}) copy-start(bf16[512,1024]{1,0:T(8,128)(2,1)} %refs_21_) | copy-start | bytes 3145732
  52.0 8.3 %copy-start.9 = (f32[16,1024]{1,0:T(8,128)}, f32[16,1024]{1,0:T(8,128)S(1)}, u32[]{:S(2)}) copy-start(f32[16,1024]{1,0:T(8,128)S(1)} %collective-permute-done.7.refs_1_.refs_6_) | copy-start | bytes 196612
  52.0 8.3 %copy-start.10 = (f32[16,1024]{1,0:T(8,128)}, f32[16,1024]{1,0:T(8,128)S(1)}, u32[]{:S(2)}) copy-start(f32[16,1024]{1,0:T(8,128)S(1)} %collective-permute-done.8.refs_3_.refs_1_.refs_8_) | copy-start | bytes 196612
  52.4 6.4 %copy-start.6 = (bf16[1024,512]{1,0:T(8,128)(2,1)}, bf16[1024,512]{1,0:T(8,128)(2,1)S(1)}, u32[]{:S(2)}) copy-start(bf16[1024,512]{1,0:T(8,128)(2,1)S(1)} %collective-permute-done.4.refs_13_) | copy-start | bytes 3145732
  52.4 45.8 %all-to-all-start = ((bf16[8,144,512]{2,1,0:T(8,128)(2,1)}), bf16[8,144,512]{2,1,0:T(8,128)(2,1)S(1)}, u32[]{:S(2)}, u32[]{:S(2)}) async-start(bf16[8,144,512]{2,1,0:T(8,128)(2,1)} %get-tuple-element.69), calls=%async_computation | async-start | bytes 2359296 | tf_op jit(solution)/shard_map/all_to_all | solution.py:893
  58.7 13.2 %collective-permute-start.9 = (bf16[1024,512]{1,0:T(8,128)(2,1)}, bf16[1024,512]{1,0:T(8,128)(2,1)S(1)}, u32[]{:S(2)}, u32[]{:S(2)}) collective-permute-start(bf16[1024,512]{1,0:T(8,128)(2,1)} %refs_13_), channel_id=1, source_target_pairs={{0,1},{1,0},{2,3},{3,2},{4,5},{5,4},{6,7},{7,6},{8,9},{9,8},{10,11... | collective-permute-start | bytes 3145736 | tf_op jit(solution)/shard_map/ppermute | solution.py:732
  59.0 39.2 %collective-permute-start.10 = (bf16[512,1024]{1,0:T(8,128)(2,1)S(1)}, bf16[512,1024]{1,0:T(8,128)(2,1)S(1)}, u32[]{:S(2)}, u32[]{:S(2)}) collective-permute-start(bf16[512,1024]{1,0:T(8,128)(2,1)S(1)} %copy-done.3), channel_id=1, source_target_pairs={{0,2},{1,3},{2,0},{3,1},{4,6},{5,7},{6,4},{7,5},{8,10},{9,11},{10,... | collective-permute-start | bytes 3145736 | tf_op jit(solution)/shard_map/ppermute | solution.py:732
  59.8 72.6 %collective-permute-start.12 = (bf16[512,1024]{1,0:T(8,128)(2,1)S(1)}, bf16[512,1024]{1,0:T(8,128)(2,1)}, u32[]{:S(2)}, u32[]{:S(2)}) collective-permute-start(bf16[512,1024]{1,0:T(8,128)(2,1)S(1)} %copy-done.3), channel_id=1, source_target_pairs={{0,1},{1,0},{2,3},{3,2},{4,5},{5,4},{6,7},{7,6},{8,9},{9,8},{10,11... | collective-permute-start | bytes 3145736 | tf_op jit(solution)/shard_map/ppermute | solution.py:732
  60.0 47.2 %collective-permute-start.11 = (bf16[1024,512]{1,0:T(8,128)(2,1)}, bf16[1024,512]{1,0:T(8,128)(2,1)}, u32[]{:S(2)}, u32[]{:S(2)}) collective-permute-start(bf16[1024,512]{1,0:T(8,128)(2,1)} %copy-done.6), channel_id=1, source_target_pairs={{0,1},{1,0},{2,3},{3,2},{4,5},{5,4},{6,7},{7,6},{8,9},{9,8},{10,11... | collective-permute-start | bytes 3145736 | tf_op jit(solution)/shard_map/ppermute | solution.py:732
  98.2 34.2 %copy-start.4 = (bf16[512,1024]{1,0:T(8,128)(2,1)}, bf16[512,1024]{1,0:T(8,128)(2,1)S(1)}, u32[]{:S(2)}) copy-start(bf16[512,1024]{1,0:T(8,128)(2,1)S(1)} %collective-permute-done.10.refs_23_) | copy-start | bytes 3145732
  98.2 34.2 %collective-permute-start.13 = (bf16[512,1024]{1,0:T(8,128)(2,1)S(1)}, bf16[512,1024]{1,0:T(8,128)(2,1)}, u32[]{:S(2)}, u32[]{:S(2)}) collective-permute-start(bf16[512,1024]{1,0:T(8,128)(2,1)S(1)} %collective-permute-done.10.refs_23_), channel_id=1, source_target_pairs={{0,1},{1,0},{2,3},{3,2},{4,5},{5,4},{6,7},{7,6},{8,9},{9,8},{10,11... | collective-permute-start | bytes 3145736 | tf_op jit(solution)/shard_map/ppermute | solution.py:732
  103.4 28.9 %all-to-all-start.1 = ((bf16[4,2,128,512]{3,2,1,0:T(8,128)(2,1)}), bf16[4,2,128,512]{3,2,1,0:T(8,128)(2,1)S(1)}, u32[]{:S(2)}, u32[]{:S(2)}) async-start(bf16[4,2,128,512]{3,2,1,0:T(8,128)(2,1)} %carries.1), calls=%async_computation.1 | async-start | bytes 2097152 | tf_op jit(solution)/shard_map/all_to_all | solution.py:1001
  (5 other events, 13.9 us)
